TPU v7x, 32 devices: a whole 2x2x4 slice. The times are simulated.
32 devices in a mesh: member: 2 (over y), band: 16 (over z, x, core).
Axes of the slice: x: 2, y: 2, z: 4, core: 2. Of those that a mesh axis runs over, the one named last changes fastest.
Arguments:
- fields: bfloat16 [4, 8192, 1024], P('member', 'band'), may hold values from -17.5 to 17.5
- w_qkv: bfloat16 [1024, 3072], replicated, may hold values from -0.1875 to 0.1875
- w_out: bfloat16 [1024, 1024], replicated, may hold values from -0.1875 to 0.1875
- decoder_weight: bfloat16 [96, 1024], replicated, may hold values from -0.1875 to 0.1875
- window_reach: int32 [16], replicated, may hold values from 1 to 128
- truth: float32 [96, 8192], P(None, 'band'), may hold values from -6 to 6
- radii: int32 [3], replicated, may hold values from 1 to 16
Outputs:
- mean_score: float32 [], replicated
- decoder_grad: float32 [96, 1024], replicated
- hidden_grad: bfloat16 [4, 8192, 1024], P('member', 'band')
All inputs are finite; a program needn't handle non-finite values.
Results may differ from a plain program's by a relative error of at most 0.012.
The roundings to bfloat16 on the way count: a program that leaves them out, or rounds other values in their place, can miss the bound.
Values may be sent and summed in bfloat16 or wider, within the bound.
No kernel may reach another device: no remote copies, remote signals or barrier semaphores. Data moves between devices by JAX's collectives and lax.ppermute only.
A program may use at most 192 MiB of HBM per device.

v0:
```python
import functools
import math

import jax
import jax.numpy as jnp
from jax import lax
from jax.experimental import pallas as pl
from jax.experimental.pallas import tpu as pltpu
from jax.sharding import PartitionSpec as P

WIN = 128
RMAX = 16
MARGIN = 2 * RMAX
HALO = WIN + MARGIN
LANES = 128
KEYS = 3 * LANES
EDGE = HALO
SUB = EDGE // 2
FRAME = EDGE + 2 * WIN
SCORE_ROWS = 144
SOFT = 0.1 * 0.1
F32 = jnp.float32
BF16 = jnp.bfloat16
NEG = -1e30
NT = (((1,), (1,)), ((), ()))
TN = (((0,), (0,)), ((), ()))


def mm(a, b):
    return jnp.dot(a, b, preferred_element_type=F32)


def half_masks():
    lane = lax.broadcasted_iota(jnp.int32, (1, LANES), 1)
    low = jnp.where(lane < LANES // 2, 1.0, 0.0).astype(BF16)
    return low, (1.0 - low.astype(F32)).astype(BF16)


def put_keys(kz, m, p, rows, piece):
    for h, mask in enumerate(half_masks()):
        kz[m, p, h, rows, :] = piece * mask


def put_values(vz, m, p, rows, piece):
    for h, mask in enumerate(half_masks()):
        vz[m, p, h, rows, :LANES] = piece * mask


def put_ones(vz, pairs):
    shape = vz.shape[:2] + vz.shape[3:4] + (LANES,)
    for h, mask in enumerate(half_masks()):
        vz[:, :, h, :, LANES:] = jnp.broadcast_to(mask.reshape(1, 1, 1, LANES), shape)


def attend(q, kz, vz, m, p, start, offset, reach, valid):
    rows = q.shape[0]
    window = pl.ds(start, KEYS)
    keys = jnp.concatenate([kz[m, p, 0, window, :], kz[m, p, 1, window, :]], axis=0)
    values = jnp.concatenate([vz[m, p, 0, window, :], vz[m, p, 1, window, :]], axis=0)
    logits = lax.dot_general(q, keys, NT, preferred_element_type=F32)
    qpos = lax.broadcasted_iota(jnp.int32, (rows, KEYS), 0) + offset
    kpos = lax.broadcasted_iota(jnp.int32, (rows, KEYS), 1)
    away = jnp.abs(qpos - kpos)
    if valid is not None:
        low, high = valid
        away = jnp.where((kpos >= low) & (kpos < high), away, 1 << 20)
    parts = []
    for h in range(2):
        one = jnp.where(away <= reach[h], logits[:, h * KEYS : (h + 1) * KEYS], NEG)
        peak = jnp.max(one, axis=1, keepdims=True)
        parts.append(jnp.exp(one - peak).astype(BF16))
    mixed = mm(jnp.concatenate(parts, axis=1), values)
    return (mixed[:, :LANES] / mixed[:, LANES:]).astype(BF16)


def main_kernel(scale, info, x, xh, wq, wk, wv, wo, dec, q_out, k_out, v_out, hid, fc, kz, vz, qs, att, res):
    step = pl.program_id(0)
    members, own, width = x.shape
    cols = wq.shape[1]
    pairs = cols // LANES
    core = info[0]
    lower = core == 1
    halo_at = jnp.where(lower, 0, HALO + own)
    near = jnp.where(lower, WIN, 0)
    edge = jnp.where(lower, 0, own - WIN + MARGIN)

    @pl.when(step == 0)
    def _():
        put_ones(vz, pairs)

    flat = x[...].reshape(members * own, width)
    flat_halo = xh[...].reshape(members * HALO, width)
    k_own = mm(flat, wk[...]).astype(BF16)
    k_halo = mm(flat_halo, wk[...]).astype(BF16)
    v_own = mm(flat, wv[...]).astype(BF16)
    v_halo = mm(flat_halo, wv[...]).astype(BF16)
    q_own = mm(flat, wq[...]).astype(BF16)
    near_rows = jnp.concatenate(
        [xh[m, pl.ds(pl.multiple_of(near, 32), MARGIN), :] for m in range(members)], axis=0
    )
    q_halo = mm(near_rows, wq[...]).astype(BF16)
    k_out[...] = k_own.reshape(members, own, cols)
    v_out[...] = v_own.reshape(members, own, cols)
    q_own = (q_own.astype(F32) * scale).astype(BF16)
    q_halo = (q_halo.astype(F32) * scale).astype(BF16)
    q_out[...] = q_own.reshape(members, own, cols)
    own_rows = pl.ds(HALO, own)
    halo_rows = pl.ds(pl.multiple_of(halo_at, 32), HALO)
    q_at = pl.ds(pl.multiple_of(halo_at + near, 32), MARGIN)
    for m in range(members):
        qs[m, own_rows, :] = q_own[m * own : (m + 1) * own]
        qs[m, q_at, :] = q_halo[m * MARGIN : (m + 1) * MARGIN]
        for p in range(pairs):
            lanes = slice(p * LANES, (p + 1) * LANES)
            put_keys(kz, m, p, own_rows, k_own[m * own : (m + 1) * own, lanes])
            put_keys(kz, m, p, halo_rows, k_halo[m * HALO : (m + 1) * HALO, lanes])
            put_values(vz, m, p, own_rows, v_own[m * own : (m + 1) * own, lanes])
            put_values(vz, m, p, halo_rows, v_halo[m * HALO : (m + 1) * HALO, lanes])

    inner = own - 2 * WIN
    for p in range(pairs):
        reach = [info[4 + (step * pairs + p) * 2 + h] for h in range(2)]
        lanes = slice(p * LANES, (p + 1) * LANES)
        out_lanes = pl.ds(pl.multiple_of(step * cols + p * LANES, LANES), LANES)
        for m in range(members):
            for b in range(inner // WIN):
                first = HALO + WIN + b * WIN
                q = qs[m, first : first + WIN, lanes]
                att[m, b * WIN : (b + 1) * WIN, out_lanes] = attend(
                    q, kz, vz, m, p, first - WIN, WIN, reach, None
                )
            for b in range(2):
                q_rows = pl.ds(pl.multiple_of(edge + WIN + b * SUB, 16), SUB)
                q = qs[m, q_rows, lanes]
                start = pl.multiple_of(edge + b * (FRAME - KEYS), 32)
                att[m, inner + b * SUB : inner + (b + 1) * SUB, out_lanes] = attend(
                    q, kz, vz, m, p, start, WIN + b * (SUB + KEYS - FRAME), reach, None
                )

    @pl.when(step == pl.num_programs(0) - 1)
    def _():
        own_first = jnp.where(lower, MARGIN, 0)
        from_own = pl.ds(pl.multiple_of(jnp.where(lower, 0, own - WIN), 32), WIN)
        for m in range(members):
            res[pl.ds(pl.multiple_of(own_first, 32), WIN), :] = x[m, from_own, :]
            res[pl.ds(pl.multiple_of(jnp.where(lower, 0, WIN), 32), MARGIN), :] = xh[
                m, pl.ds(pl.multiple_of(near, 32), MARGIN), :
            ]
            mixed = mm(att[m], wo[...])
            hid[m, :inner, :] = (mixed[:inner] + x[m, WIN : own - WIN, :].astype(F32)).astype(BF16)
            hid[m, inner:, :] = (mixed[inner:] + res[...].astype(F32)).astype(BF16)
            fc[m] = lax.dot_general(hid[m], dec[...], NT, preferred_element_type=F32)


def edge_kernel(scale, info, x, xh, wq, wk, wv, qi, ki, vi, wo, dec, hid, fc, kz, vz, qs, att, res):
    step = pl.program_id(0)
    members, own, width = x.shape
    cols = wq.shape[1]
    pairs = cols // LANES
    lower = info[0] == 0
    halo_at = jnp.where(lower, 0, 2 * WIN)
    own_at = jnp.where(lower, HALO, 0)
    near = jnp.where(lower, WIN, 0)
    low = jnp.where(info[1] == 1, HALO, 0)
    high = jnp.where(info[2] == 1, 2 * WIN, FRAME)

    @pl.when(step == 0)
    def _():
        put_ones(vz, pairs)

    flat_halo = xh[...].reshape(members * HALO, width)
    k_halo = mm(flat_halo, wk[...]).astype(BF16)
    v_halo = mm(flat_halo, wv[...]).astype(BF16)
    near_rows = jnp.concatenate(
        [xh[m, pl.ds(pl.multiple_of(near, 32), MARGIN), :] for m in range(members)], axis=0
    )
    q_halo = mm(near_rows, wq[...]).astype(BF16)
    q_halo = (q_halo.astype(F32) * scale).astype(BF16)
    own_rows = pl.ds(pl.multiple_of(own_at, 32), 2 * WIN)
    halo_rows = pl.ds(pl.multiple_of(halo_at, 32), HALO)
    for m in range(members):
        qs[m, pl.ds(pl.multiple_of(jnp.where(lower, MARGIN, 0), 32), WIN), :] = qi[m]
        qs[m, pl.ds(pl.multiple_of(jnp.where(lower, 0, WIN), 32), MARGIN), :] = q_halo[
            m * MARGIN : (m + 1) * MARGIN
        ]
        for p in range(pairs):
            lanes = slice(p * LANES, (p + 1) * LANES)
            put_keys(kz, m, p, own_rows, ki[m, :, lanes])
            put_keys(kz, m, p, halo_rows, k_halo[m * HALO : (m + 1) * HALO, lanes])
            put_values(vz, m, p, own_rows, vi[m, :, lanes])
            put_values(vz, m, p, halo_rows, v_halo[m * HALO : (m + 1) * HALO, lanes])

    for p in range(pairs):
        reach = [info[4 + (step * pairs + p) * 2 + h] for h in range(2)]
        lanes = slice(p * LANES, (p + 1) * LANES)
        out_lanes = pl.ds(pl.multiple_of(step * cols + p * LANES, LANES), LANES)
        for m in range(members):
            for b in range(2):
                start = b * (FRAME - KEYS)
                att[m, b * SUB : (b + 1) * SUB, out_lanes] = attend(
                    qs[m, b * SUB : (b + 1) * SUB, lanes],
                    kz,
                    vz,
                    m,
                    p,
                    start,
                    WIN + b * SUB - start,
                    reach,
                    (low - start, high - start),
                )

    @pl.when(step == pl.num_programs(0) - 1)
    def _():
        from_own = pl.ds(pl.multiple_of(jnp.where(lower, 0, own - WIN), 32), WIN)
        for m in range(members):
            res[m, pl.ds(pl.multiple_of(jnp.where(lower, MARGIN, 0), 32), WIN), :] = x[m, from_own, :]
            res[m, pl.ds(pl.multiple_of(jnp.where(lower, 0, WIN), 32), MARGIN), :] = xh[
                m, pl.ds(pl.multiple_of(near, 32), MARGIN), :
            ]
        mixed = mm(att[...].reshape(members * EDGE, width), wo[...])
        hidden = (mixed + res[...].reshape(members * EDGE, width).astype(F32)).astype(BF16)
        hid[...] = hidden.reshape(members, EDGE, width)
        fc[...] = lax.dot_general(hidden, dec[...], NT, preferred_element_type=F32).reshape(
            members, EDGE, dec.shape[0]
        )


def toeplitz(radii, scale_index, rows, cols):
    reach = radii[scale_index].astype(F32)
    spread = 0.5 * reach
    twice = 2.0 * spread * spread

    def weigh(shape, shift):
        away = lax.broadcasted_iota(jnp.int32, shape, 1) - shift
        far = jnp.abs(away).astype(F32)
        return jnp.where(far <= reach, jnp.exp(-(far * far) / twice), 0.0)

    line = weigh((8, LANES), RMAX)
    total = jnp.sum(line, axis=1, keepdims=True)[:1]
    shift = lax.broadcasted_iota(jnp.int32, (rows, cols), 0) + RMAX
    return weigh((rows, cols), shift) / total


def split(values):
    high = values.astype(BF16)
    return high, (values - high.astype(F32)).astype(BF16)


def score_kernel(
    channels, members_total, info, radii, fa, fb, ga, gb, truth, t_near, t_far, hid_a, hid_b, cot, part, fh, fl, sh, sl
):
    members, _, _ = fa.shape
    own = truth.shape[0]
    scales = radii.shape[0]
    inner = own - 2 * WIN
    rows = SCORE_ROWS
    window = 2 * LANES
    lower = info[0] == 0
    begins, ends = info[1] == 1, info[2] == 1
    far_at = pl.ds(pl.multiple_of(jnp.where(lower, 0, inner + EDGE), 32), EDGE)
    near_at = pl.ds(pl.multiple_of(jnp.where(lower, inner + EDGE, 0), 32), EDGE)
    total_rows = own + 2 * MARGIN

    def put(at, column, values):
        lanes = slice(column * LANES, (column + 1) * LANES)
        fh[at, lanes], fl[at, lanes] = split(values)

    for side, (f_main, f_far) in enumerate(((fa, fb), (ga, gb))):
        for m in range(members):
            column = side * members + m
            put(pl.ds(EDGE, inner), column, f_main[m, :inner, :])
            put(near_at, column, f_main[m, inner:, :])
            put(far_at, column, f_far[m])
    put(pl.ds(MARGIN, own), 2 * members, truth[...])
    put(pl.ds(pl.multiple_of(jnp.where(lower, 0, MARGIN + own), 32), MARGIN), 2 * members, t_far[...])
    put(pl.ds(pl.multiple_of(jnp.where(lower, MARGIN + own, 0), 32), MARGIN), 2 * members, t_near[...])
    for ref in (fh, fl):
        ref[total_rows:, :] = jnp.zeros((ref.shape[0] - total_rows, ref.shape[1]), BF16)

        @pl.when(begins)
        def _():
            ref[:MARGIN, :] = jnp.zeros((MARGIN, ref.shape[1]), BF16)

        @pl.when(ends)
        def _():
            ref[MARGIN + own : total_rows, :] = jnp.zeros((MARGIN, ref.shape[1]), BF16)

    tiles = -(-(own + 2 * RMAX) // rows)
    for ref in (sh, sl):
        spare = ref.shape[1] - tiles * rows
        ref[:, tiles * rows :, :] = jnp.zeros((scales, spare, ref.shape[2]), BF16)

    weights = [split(toeplitz(radii, s, rows, window)) for s in range(scales)]
    forward = jnp.concatenate([jnp.concatenate([h, h, l], axis=1) for h, l in weights], axis=0)
    backward = jnp.concatenate(
        [h[:LANES] for h, l in weights] + [h[:LANES] for h, l in weights] + [l[:LANES] for h, l in weights],
        axis=1,
    )
    first_valid = jnp.where(begins, RMAX, 0)
    last_valid = jnp.where(ends, RMAX + own, 2 * RMAX + own)
    pair_weight = 1.0 / (members_total * (members_total - 1))
    others = 2 * members
    total = jnp.zeros((rows, LANES), F32)
    for tile in range(tiles):
        at = pl.ds(tile * rows, window)
        stacked = jnp.concatenate([fh[at, :], fl[at, :], fh[at, :]], axis=0)
        smooth = mm(forward, stacked)
        line = lax.broadcasted_iota(jnp.int32, (rows, LANES), 0) + tile * rows
        valid = jnp.where((line >= first_valid) & (line < last_valid), 1.0, 0.0)
        tile_score = jnp.zeros((rows, LANES), F32)
        for s in range(scales):
            values = [
                smooth[s * rows : (s + 1) * rows, i * LANES : (i + 1) * LANES] for i in range(others + 1)
            ]

            def gap(a, b):
                away = values[a] - values[b]
                square = away * away + SOFT
                inverse = lax.rsqrt(square)
                return away * inverse, square * inverse

            skill = jnp.zeros((rows, LANES), F32)
            spread = jnp.zeros((rows, LANES), F32)
            slopes = []
            cross = [jnp.zeros((rows, LANES), F32) for _ in range(members)]
            for m in range(members):
                slope, size = gap(m, others)
                skill = skill + size
                slopes.append(slope)
            for a in range(members):
                for b in range(a + 1, others):
                    slope, size = gap(a, b)
                    cross[a] = cross[a] + slope
                    if b < members:
                        cross[b] = cross[b] - slope
                        spread = spread + size
                    else:
                        spread = spread + 0.5 * size
            tile_score = tile_score + (skill * (1.0 / members_total) - pair_weight * spread)
            for m in range(members):
                slope = (slopes[m] * (1.0 / members_total) - pair_weight * cross[m]) * valid
                keep, lanes = pl.ds(tile * rows, rows), slice(m * LANES, (m + 1) * LANES)
                sh[s, keep, lanes], sl[s, keep, lanes] = split(slope)
        mine = (line >= RMAX) & (line < RMAX + own)
        total = total + jnp.where(mine, tile_score, 0.0)
    lane = lax.broadcasted_iota(jnp.int32, (rows, LANES), 1)
    total = jnp.where(lane < channels, total, 0.0)
    score = jnp.sum(jnp.sum(total, axis=0, keepdims=True), axis=1, keepdims=True)

    for tile in range(own // LANES):
        at = pl.ds(tile * LANES, window)
        high = [sh[s, at, :] for s in range(scales)]
        low = [sl[s, at, :] for s in range(scales)]
        stacked = jnp.concatenate(high + low + high, axis=0)
        cot[tile * LANES : (tile + 1) * LANES, :] = mm(backward, stacked).astype(BF16)

    near_own = pl.ds(pl.multiple_of(jnp.where(lower, own - WIN, 0), 32), WIN)
    far_own = pl.ds(pl.multiple_of(jnp.where(lower, 0, own - WIN), 32), WIN)
    near_skip = pl.multiple_of(jnp.where(lower, 0, MARGIN), 32)
    far_skip = pl.multiple_of(jnp.where(lower, MARGIN, 0), 32)
    width = hid_a.shape[2]
    grad = jnp.zeros((LANES, width), F32)
    for m in range(members):
        lanes = slice(m * LANES, (m + 1) * LANES)
        for c_rows, ref, h_rows in (
            (pl.ds(WIN, inner), hid_a, pl.ds(0, inner)),
            (near_own, hid_a, pl.ds(inner + near_skip, WIN)),
            (far_own, hid_b, pl.ds(far_skip, WIN)),
        ):
            grad = grad + lax.dot_general(cot[c_rows, lanes], ref[m, h_rows, :], TN, preferred_element_type=F32)
    keep = part.shape[1]
    line = lax.broadcasted_iota(jnp.int32, (keep, LANES), 0)
    score_high = score.astype(BF16).astype(F32)
    extra = jnp.where(line == channels, score_high, score - score_high)
    for chunk in range(width // LANES):
        piece = grad[:keep, chunk * LANES : (chunk + 1) * LANES]
        part[chunk] = jnp.where(line < channels, piece, jnp.where(line < channels + 2, extra, 0.0)).astype(BF16)


def grad_kernel(cot, dec, out):
    out[0] = mm(cot[...], dec[...]).astype(BF16)


def swap_pairs(count, first):
    pairs = []
    for i in range(first, count - 1, 2):
        pairs += [(i, i + 1), (i + 1, i)]
    return pairs


def reduce_all(part, mesh_shape):
    bands, count = mesh_shape["band"], mesh_shape["member"]
    half = part.shape[0] // 2
    core = lax.axis_index("band") % 2

    def swap(values, axis, size, bit):
        return lax.ppermute(values, axis, [(i, i ^ bit) for i in range(size)])

    mine = lax.dynamic_slice_in_dim(part, core * half, half, 0)
    theirs = lax.dynamic_slice_in_dim(part, (1 - core) * half, half, 0)
    total = mine.astype(F32) + swap(theirs, "band", bands, 1).astype(F32)
    bit = 1
    while bit < count:
        total = total + swap(total.astype(BF16), "member", count, bit).astype(F32)
        bit *= 2
    bit = 2
    while bit < bands:
        total = total + swap(total.astype(BF16), "band", bands, bit).astype(F32)
        bit *= 2
    other = swap(total.astype(BF16), "band", bands, 1).astype(F32)
    first = jnp.where(core == 0, total, other)
    second = jnp.where(core == 0, other, total)
    return jnp.concatenate([first, second], axis=0)


def local(mesh_shape, fields, w_qkv, w_out, decoder_weight, window_reach, truth, radii):
    members, own, width = fields.shape
    heads = window_reach.shape[0]
    head = width // heads
    channels = decoder_weight.shape[0]
    scales = radii.shape[0]
    bands, member_count = mesh_shape["band"], mesh_shape["member"]
    members_total = members * member_count
    scale = head**-0.5
    band = lax.axis_index("band")
    core = band % 2
    info = jnp.concatenate(
        [
            jnp.stack([core, band == 0, band == bands - 1, 0]).astype(jnp.int32),
            window_reach.astype(jnp.int32),
        ]
    )
    inside, across = swap_pairs(bands, 0), swap_pairs(bands, 1)

    def exchange(block, dim, size):
        last = block.shape[dim] - size
        near = lax.dynamic_slice_in_dim(block, (1 - core) * last, size, dim)
        far = lax.dynamic_slice_in_dim(block, core * last, size, dim)
        return lax.ppermute(near, "band", inside), lax.ppermute(far, "band", across)

    x_near, x_far = exchange(fields, 1, HALO)
    truth_t = jnp.pad(truth.T, ((0, 0), (0, LANES - channels)))
    t_near, t_far = exchange(truth_t, 0, MARGIN)
    dec = jnp.pad(decoder_weight, ((0, LANES - channels), (0, 0)))

    cols = 2 * LANES
    steps = width // cols
    pairs = cols // LANES
    whole = lambda shape: pl.BlockSpec(shape, lambda i, s: (0,) * len(shape))
    weight = lambda third: pl.BlockSpec((width, cols), lambda i, s: (0, third * steps + i))
    inner = own - 2 * WIN
    main_rows = inner + EDGE
    col_block = lambda rows: pl.BlockSpec((members, rows, cols), lambda i, s: (0, 0, i))
    params = pltpu.CompilerParams(
        dimension_semantics=("arbitrary",), vmem_limit_bytes=48 * 1024 * 1024
    )
    q_own, k_own, v_own, hid_a, fc_a = pl.pallas_call(
        functools.partial(main_kernel, scale),
        grid_spec=pltpu.PrefetchScalarGridSpec(
            num_scalar_prefetch=1,
            grid=(steps,),
            in_specs=[
                whole((members, own, width)),
                whole((members, HALO, width)),
                weight(0),
                weight(1),
                weight(2),
                whole((width, width)),
                whole((LANES, width)),
            ],
            out_specs=[
                col_block(own),
                col_block(own),
                col_block(own),
                whole((members, main_rows, width)),
                whole((members, main_rows, LANES)),
            ],
            scratch_shapes=[
                pltpu.VMEM((members, pairs, 2, own + 2 * HALO, LANES), BF16),
                pltpu.VMEM((members, pairs, 2, own + 2 * HALO, 2 * LANES), BF16),
                pltpu.VMEM((members, own + 2 * HALO, cols), BF16),
                pltpu.VMEM((members, main_rows, width), BF16),
                pltpu.VMEM((EDGE, width), BF16),
            ],
        ),
        out_shape=[jax.ShapeDtypeStruct((members, own, width), BF16)] * 3
        + [
            jax.ShapeDtypeStruct((members, main_rows, width), BF16),
            jax.ShapeDtypeStruct((members, main_rows, LANES), F32),
        ],
        compiler_params=params,
        cost_estimate=pl.CostEstimate(
            flops=2 * members * own * width * 5 * width, bytes_accessed=24 << 20, transcendentals=1 << 22
        ),
    )(info, fields, x_near, w_qkv, w_qkv, w_qkv, w_out, dec)

    member_pairs = [(i, i ^ 1) for i in range(member_count)]
    other_a = lax.ppermute(fc_a, "member", member_pairs)

    far_block = lambda rows, last: pl.BlockSpec((members, rows, cols), lambda i, s: (0, s[0] * last, i))
    hid_b, fc_b = pl.pallas_call(
        functools.partial(edge_kernel, scale),
        grid_spec=pltpu.PrefetchScalarGridSpec(
            num_scalar_prefetch=1,
            grid=(steps,),
            in_specs=[
                whole((members, own, width)),
                whole((members, HALO, width)),
                weight(0),
                weight(1),
                weight(2),
                far_block(WIN, own // WIN - 1),
                far_block(2 * WIN, own // (2 * WIN) - 1),
                far_block(2 * WIN, own // (2 * WIN) - 1),
                whole((width, width)),
                whole((LANES, width)),
            ],
            out_specs=[whole((members, EDGE, width)), whole((members, EDGE, LANES))],
            scratch_shapes=[
                pltpu.VMEM((members, pairs, 2, FRAME, LANES), BF16),
                pltpu.VMEM((members, pairs, 2, FRAME, 2 * LANES), BF16),
                pltpu.VMEM((members, EDGE, cols), BF16),
                pltpu.VMEM((members, EDGE, width), BF16),
                pltpu.VMEM((members, EDGE, width), BF16),
            ],
        ),
        out_shape=[
            jax.ShapeDtypeStruct((members, EDGE, width), BF16),
            jax.ShapeDtypeStruct((members, EDGE, LANES), F32),
        ],
        compiler_params=params,
        cost_estimate=pl.CostEstimate(
            flops=2 * members * own * width * 2 * width, bytes_accessed=14 << 20, transcendentals=1 << 21
        ),
    )(info, fields, x_far, w_qkv, w_qkv, w_qkv, q_own, k_own, v_own, w_out, dec)
    other_b = lax.ppermute(fc_b, "member", member_pairs)

    keep = channels + 16
    chunks = width // LANES
    tiles = -(-(own + 2 * RMAX) // SCORE_ROWS)
    f_rows = (tiles - 1) * SCORE_ROWS + 2 * LANES
    s_rows = own + LANES
    smem = pl.BlockSpec(memory_space=pltpu.SMEM)
    vmem = pl.BlockSpec(memory_space=pltpu.VMEM)
    cot, part = pl.pallas_call(
        functools.partial(score_kernel, channels, members_total),
        in_specs=[smem, smem] + [vmem] * 9,
        out_specs=[vmem, vmem],
        out_shape=[
            jax.ShapeDtypeStruct((own, members * LANES), BF16),
            jax.ShapeDtypeStruct((chunks, keep, LANES), BF16),
        ],
        scratch_shapes=[
            pltpu.VMEM((f_rows, (2 * members + 1) * LANES), BF16),
            pltpu.VMEM((f_rows, (2 * members + 1) * LANES), BF16),
            pltpu.VMEM((scales, s_rows, members * LANES), BF16),
            pltpu.VMEM((scales, s_rows, members * LANES), BF16),
        ],
        compiler_params=pltpu.CompilerParams(vmem_limit_bytes=48 * 1024 * 1024),
    )(info, radii, fc_a, fc_b, other_a, other_b, truth_t, t_near, t_far, hid_a, hid_b)

    hidden_grad = pl.pallas_call(
        grad_kernel,
        grid=(members, 2),
        in_specs=[
            pl.BlockSpec((own // 2, LANES), lambda m, h: (h, m)),
            pl.BlockSpec((LANES, width), lambda m, h: (0, 0)),
        ],
        out_specs=pl.BlockSpec((1, own // 2, width), lambda m, h: (m, h, 0)),
        out_shape=jax.ShapeDtypeStruct((members, own, width), BF16),
        cost_estimate=pl.CostEstimate(
            flops=2 * members * own * LANES * width, bytes_accessed=3 << 20, transcendentals=0
        ),
    )(cot, dec)

    summed = reduce_all(part, mesh_shape)
    decoder_grad = summed[:, :channels, :].transpose(1, 0, 2).reshape(channels, width)
    decoder_grad = decoder_grad / math.sqrt(members_total * own * bands)
    mean_score = (summed[0, channels, 0] + summed[0, channels + 1, 0]) / (scales * channels * own * bands)
    return (mean_score, decoder_grad, hidden_grad)


def solution(mesh):
    placed = (P("member", "band", None), P(), P(), P(), P(), P(None, "band"), P())
    return jax.shard_map(
        functools.partial(local, dict(mesh.shape)),
        mesh=mesh,
        in_specs=placed,
        out_specs=(P(), P(), P("member", "band", None)),
        check_vma=False,
    )
```

profile of v0, /device:TPU:25, one launch (start us, length us, event | category | flops | bytes accessed | tf_op | source)
XLA Modules:
  0.0 99.2 jit_solution(12630704898291115090)
XLA Ops:
  0.7 2.3 %constant_dynamic-slice_fusion.3 = (bf16[2,160,1024]{2,1,0:T(8,128)(2,1)}, bf16[2,160,1024]{2,1,0:T(8,128)(2,1)S(1)}) fusion(bf16[2,512,1024]{2,1,0:T(8,128)(2,1)} %x.7, s32[]{:T(128)S(6)} %select_n.42, s32[]{:T(128)S(6)} %select_n.41), kind=kLoop, calls=%fused_computation.17 | loop fusion | bytes 2621448 | tf_op jit(solution)/shard_map/dynamic_slice | solution.py:438
  3.0 0.7 collective-permute-start
  3.7 3.0 %collective-permute-start.1 = (bf16[2,160,1024]{2,1,0:T(8,128)(2,1)}, bf16[2,160,1024]{2,1,0:T(8,128)(2,1)S(1)}, u32[]{:S(2)}, u32[]{:S(2)}) collective-permute-start(bf16[2,160,1024]{2,1,0:T(8,128)(2,1)} %get-tuple-element.23), channel_id=1, source_target_pairs={{1,2},{2,1},{3,4},{4,3},{5,6},{6,5},{7,8},{8,7},{9,10},{10,9},{11,... | collective-permute-start | bytes 1966088 | tf_op jit(solution)/shard_map/ppermute | solution.py:439
  6.7 0.1 concatenate.6.info
  6.8 31.9 %shard_map.94 = (bf16[2,512,1024]{2,1,0:T(8,128)(2,1)S(1)}, bf16[2,512,1024]{2,1,0:T(8,128)(2,1)}, bf16[2,512,1024]{2,1,0:T(8,128)(2,1)}, bf16[2,416,1024]{2,1,0:T(8,128)(2,1)S(1)}, f32[2,416,128]{2,1,0:T(8,128)}) custom-call(s32[20]{0:T(128)S(1)} %concatenate.6.info, bf16[2,512,1024]{2,1,0:T(8,128)(2,1)} %x.7, ...), custom_call_target="tpu_custom_call" | custom-call | flops 10737418240 | bytes 25165824 | tf_op jit(solution)/shard_map/pallas_call | solution.py:457
  38.7 1.3 %collective-permute-start.2 = (f32[2,416,128]{2,1,0:T(8,128)}, f32[2,416,128]{2,1,0:T(8,128)}, u32[]{:S(2)}, u32[]{:S(2)}) collective-permute-start(f32[2,416,128]{2,1,0:T(8,128)} %get-tuple-element.12.fa), channel_id=1, source_target_pairs={{0,16},{16,0},{1,17},{17,1},{2,18},{18,2},{3,19},{19,3},{4,20},{20... | collective-permute-start | bytes 1277960 | tf_op jit(solution)/shard_map/ppermute | solution.py:498
  40.0 12.9 %shard_map.95 = (bf16[2,160,1024]{2,1,0:T(8,128)(2,1)S(1)}, f32[2,160,128]{2,1,0:T(8,128)}) custom-call(s32[20]{0:T(128)S(1)} %concatenate.6.info, bf16[2,512,1024]{2,1,0:T(8,128)(2,1)S(1)} %copy-done, bf16[2,160,1024]{2,1,0:T(8,128)(2,1)S(1)} %collective-permute-done.1.xh, bf16[1024,3072]{1,0:T(8,128)(2,1)} %wv.3, bf16[1024,3072]{1,0:T(8,128)(2,1)} %wv.3, ...), custom_call_target="tpu_custom_call" | custom-call | flops 4294967296 | bytes 14680064 | tf_op jit(solution)/shard_map/pallas_call | solution.py:501
  52.9 0.2 collective-permute-start.3
  53.1 0.1 copy.11
  53.3 1.1 %collective-permute-start.4 = (f32[32,128]{1,0:T(8,128)S(1)}, f32[32,128]{1,0:T(8,128)S(1)}, u32[]{:S(2)}, u32[]{:S(2)}) collective-permute-start(f32[32,128]{1,0:T(8,128)S(1)} %get-tuple-element.28), channel_id=1, source_target_pairs={{0,1},{1,0},{2,3},{3,2},{4,5},{5,4},{6,7},{7,6},{8,9},{9,8},{10,11... | collective-permute-start | bytes 49160 | tf_op jit(solution)/shard_map/ppermute | solution.py:439
  54.4 2.2 %collective-permute-start.5 = (f32[32,128]{1,0:T(8,128)S(1)}, f32[32,128]{1,0:T(8,128)S(1)}, u32[]{:S(2)}, u32[]{:S(2)}) collective-permute-start(f32[32,128]{1,0:T(8,128)S(1)} %get-tuple-element.27), channel_id=1, source_target_pairs={{1,2},{2,1},{3,4},{4,3},{5,6},{6,5},{7,8},{8,7},{9,10},{10,9},{11,... | collective-permute-start | bytes 49160 | tf_op jit(solution)/shard_map/ppermute | solution.py:439
  56.6 3.1 %collective-permute-done.5.t_far = f32[32,128]{1,0:T(8,128)S(1)} collective-permute-done((f32[32,128]{1,0:T(8,128)S(1)}, f32[32,128]{1,0:T(8,128)S(1)}, u32[]{:S(2)}, u32[]{:S(2)}) %collective-permute-start.5) | collective-permute-done | bytes 16416 | tf_op jit(solution)/shard_map/ppermute | solution.py:439
  59.7 6.7 %shard_map.96 = (bf16[512,256]{1,0:T(8,128)(2,1)S(1)}, bf16[8,112,128]{2,1,0:T(8,128)(2,1)S(1)}) custom-call(s32[20]{0:T(128)S(1)} %concatenate.6.info, s32[3]{0:T(128)S(1)} %copy-done.3, f32[2,416,128]{2,1,0:T(8,128)} %get-tuple-element.12.fa, f32[2,160,128]{2,1,0:T(8,128)} %get-tuple-element.16.fb, f32[2,416,128]{2,1,0:T(8,128)} %collective-permute-done.2.ga, ...), custom_call_target="tpu_custom_call" | custom-call | tf_op jit(solution)/shard_map/pallas_call | solution.py:545
  66.4 0.7 copy-done.2
  67.1 0.7 collective-permute-start.6
  67.8 1.0 collective-permute-done.6
  68.8 1.3 %collective-permute-start.7 = (bf16[4,112,128]{2,1,0:T(8,128)(2,1)S(1)}, bf16[4,112,128]{2,1,0:T(8,128)(2,1)S(1)}, u32[]{:S(2)}, u32[]{:S(2)}) collective-permute-start(bf16[4,112,128]{2,1,0:T(8,128)(2,1)S(1)} %fusion.2), channel_id=1, source_target_pairs={{0,16},{16,0},{1,17},{17,1},{2,18},{18,2},{3,19},{19,3},{4,20},{20... | collective-permute-start | bytes 344072 | tf_op jit(solution)/shard_map/ppermute | solution.py:397
  70.1 3.1 %collective-permute-done.7 = bf16[4,112,128]{2,1,0:T(8,128)(2,1)S(1)} collective-permute-done((bf16[4,112,128]{2,1,0:T(8,128)(2,1)S(1)}, bf16[4,112,128]{2,1,0:T(8,128)(2,1)S(1)}, u32[]{:S(2)}, u32[]{:S(2)}) %collective-permute-start.7) | collective-permute-done | bytes 114720 | tf_op jit(solution)/shard_map/ppermute | solution.py:397
  73.2 0.1 fusion.5
  73.3 0.1 collective-permute-start.8
  73.4 3.6 %collective-permute-done.8 = bf16[4,112,128]{2,1,0:T(8,128)(2,1)S(1)} collective-permute-done((bf16[4,112,128]{2,1,0:T(8,128)(2,1)S(1)}, bf16[4,112,128]{2,1,0:T(8,128)(2,1)S(1)}, u32[]{:S(2)}, u32[]{:S(2)}) %collective-permute-start.8) | collective-permute-done | bytes 114720 | tf_op jit(solution)/shard_map/ppermute | solution.py:397
  77.0 0.1 fusion.3
  77.1 0.2 collective-permute-start.9
  77.3 3.5 %collective-permute-done.9 = bf16[4,112,128]{2,1,0:T(8,128)(2,1)S(1)} collective-permute-done((bf16[4,112,128]{2,1,0:T(8,128)(2,1)S(1)}, bf16[4,112,128]{2,1,0:T(8,128)(2,1)S(1)}, u32[]{:S(2)}, u32[]{:S(2)}) %collective-permute-start.9) | collective-permute-done | bytes 114720 | tf_op jit(solution)/shard_map/ppermute | solution.py:397
  80.8 0.1 fusion.4
  80.9 0.1 collective-permute-start.10
  81.0 5.6 %collective-permute-done.10 = bf16[4,112,128]{2,1,0:T(8,128)(2,1)S(1)} collective-permute-done((bf16[4,112,128]{2,1,0:T(8,128)(2,1)S(1)}, bf16[4,112,128]{2,1,0:T(8,128)(2,1)S(1)}, u32[]{:S(2)}, u32[]{:S(2)}) %collective-permute-start.10) | collective-permute-done | bytes 114720 | tf_op jit(solution)/shard_map/ppermute | solution.py:397
  86.6 0.1 fusion.6
  86.7 4.8 %collective-permute-start.11 = (bf16[4,112,128]{2,1,0:T(8,128)(2,1)S(1)}, bf16[4,112,128]{2,1,0:T(8,128)(2,1)S(1)}, u32[]{:S(2)}, u32[]{:S(2)}) collective-permute-start(bf16[4,112,128]{2,1,0:T(8,128)(2,1)S(1)} %get-tuple-element.21), channel_id=1, source_target_pairs={{0,1},{1,0},{2,3},{3,2},{4,5},{5,4},{6,7},{7,6},{8,9},{9,8},{10,11... | collective-permute-start | bytes 344072 | tf_op jit(solution)/shard_map/ppermute | solution.py:397
  91.5 4.0 %shard_map.97 = bf16[2,512,1024]{2,1,0:T(8,128)(2,1)} custom-call(bf16[512,256]{1,0:T(8,128)(2,1)} %copy-done.2, bf16[128,1024]{1,0:T(8,128)(2,1)} %copy-done.1), custom_call_target="tpu_custom_call" | custom-call | flops 268435456 | bytes 3145728 | tf_op jit(solution)/shard_map/pallas_call | solution.py:562
  95.5 0.5 fusion.7
  96.0 0.8 copy_bitcast_fusion
  (25 shorter events, 0.2 us)
Async XLA Ops:
  0.6 6.1 %copy-start.5 = (bf16[96,1024]{1,0:T(8,128)(2,1)S(1)}, bf16[96,1024]{1,0:T(8,128)(2,1)}, u32[]{:S(2)}) copy-start(bf16[96,1024]{1,0:T(8,128)(2,1)} %param.10) | copy-start | bytes 589828
  0.6 6.1 %copy-start.6 = (s32[16]{0:T(128)S(1)}, s32[16]{0:T(128)}, u32[]{:S(2)}) copy-start(s32[16]{0:T(128)} %param.11) | copy-start | bytes 196
  3.0 3.8 %collective-permute-start = (bf16[2,160,1024]{2,1,0:T(8,128)(2,1)S(1)}, bf16[2,160,1024]{2,1,0:T(8,128)(2,1)S(1)}, u32[]{:S(2)}, u32[]{:S(2)}) collective-permute-start(bf16[2,160,1024]{2,1,0:T(8,128)(2,1)S(1)} %get-tuple-element.24), channel_id=1, source_target_pairs={{0,1},{1,0},{2,3},{3,2},{4,5},{5,4},{6,7},{7,6},{8,9},{9,8},{10,11... | collective-permute-start | bytes 1966088 | tf_op jit(solution)/shard_map/ppermute | solution.py:439
  3.7 36.3 %collective-permute-start.1 = (bf16[2,160,1024]{2,1,0:T(8,128)(2,1)}, bf16[2,160,1024]{2,1,0:T(8,128)(2,1)S(1)}, u32[]{:S(2)}, u32[]{:S(2)}) collective-permute-start(bf16[2,160,1024]{2,1,0:T(8,128)(2,1)} %get-tuple-element.23), channel_id=1, source_target_pairs={{1,2},{2,1},{3,4},{4,3},{5,6},{6,5},{7,8},{8,7},{9,10},{10,9},{11,... | collective-permute-start | bytes 1966088 | tf_op jit(solution)/shard_map/ppermute | solution.py:439
  6.7 33.3 %copy-start.1 = (bf16[128,1024]{1,0:T(8,128)(2,1)}, bf16[128,1024]{1,0:T(8,128)(2,1)S(1)}, u32[]{:S(2)}) copy-start(bf16[128,1024]{1,0:T(8,128)(2,1)S(1)} %pad.8.dec) | copy-start | bytes 786436
  6.8 33.2 %copy-start = (bf16[2,512,1024]{2,1,0:T(8,128)(2,1)S(1)}, bf16[2,512,1024]{2,1,0:T(8,128)(2,1)}, u32[]{:S(2)}) copy-start(bf16[2,512,1024]{2,1,0:T(8,128)(2,1)} %x.7) | copy-start | bytes 6291460
  38.7 21.0 %collective-permute-start.2 = (f32[2,416,128]{2,1,0:T(8,128)}, f32[2,416,128]{2,1,0:T(8,128)}, u32[]{:S(2)}, u32[]{:S(2)}) collective-permute-start(f32[2,416,128]{2,1,0:T(8,128)} %get-tuple-element.12.fa), channel_id=1, source_target_pairs={{0,16},{16,0},{1,17},{17,1},{2,18},{18,2},{3,19},{19,3},{4,20},{20... | collective-permute-start | bytes 1277960 | tf_op jit(solution)/shard_map/ppermute | solution.py:498
  40.0 13.1 %copy-start.4 = (f32[96,512]{1,0:T(8,128)S(1)}, f32[96,512]{1,0:T(8,128)}, u32[]{:S(2)}) copy-start(f32[96,512]{1,0:T(8,128)} %param.12) | copy-start | bytes 589828
  40.0 19.7 %copy-start.3 = (s32[3]{0:T(128)S(1)}, s32[3]{0:T(128)}, u32[]{:S(2)}) copy-start(s32[3]{0:T(128)} %radii.1) | copy-start | bytes 40
  52.9 6.8 %collective-permute-start.3 = (f32[2,160,128]{2,1,0:T(8,128)}, f32[2,160,128]{2,1,0:T(8,128)S(1)}, u32[]{:S(2)}, u32[]{:S(2)}) collective-permute-start(f32[2,160,128]{2,1,0:T(8,128)} %get-tuple-element.16.fb), channel_id=1, source_target_pairs={{0,16},{16,0},{1,17},{17,1},{2,18},{18,2},{3,19},{19,3},{4,20},{20... | collective-permute-start | bytes 491528 | tf_op jit(solution)/shard_map/ppermute | solution.py:536
  53.3 3.3 %collective-permute-start.4 = (f32[32,128]{1,0:T(8,128)S(1)}, f32[32,128]{1,0:T(8,128)S(1)}, u32[]{:S(2)}, u32[]{:S(2)}) collective-permute-start(f32[32,128]{1,0:T(8,128)S(1)} %get-tuple-element.28), channel_id=1, source_target_pairs={{0,1},{1,0},{2,3},{3,2},{4,5},{5,4},{6,7},{7,6},{8,9},{9,8},{10,11... | collective-permute-start | bytes 49160 | tf_op jit(solution)/shard_map/ppermute | solution.py:439
  54.4 5.3 %collective-permute-start.5 = (f32[32,128]{1,0:T(8,128)S(1)}, f32[32,128]{1,0:T(8,128)S(1)}, u32[]{:S(2)}, u32[]{:S(2)}) collective-permute-start(f32[32,128]{1,0:T(8,128)S(1)} %get-tuple-element.27), channel_id=1, source_target_pairs={{1,2},{2,1},{3,4},{4,3},{5,6},{6,5},{7,8},{8,7},{9,10},{10,9},{11,... | collective-permute-start | bytes 49160 | tf_op jit(solution)/shard_map/ppermute | solution.py:439
  66.4 0.7 copy-start.2
  67.1 1.7 %collective-permute-start.6 = (bf16[4,112,128]{2,1,0:T(8,128)(2,1)S(1)}, bf16[4,112,128]{2,1,0:T(8,128)(2,1)S(1)}, u32[]{:S(2)}, u32[]{:S(2)}) collective-permute-start(bf16[4,112,128]{2,1,0:T(8,128)(2,1)S(1)} %constant_dynamic-slice_fusion), channel_id=1, source_target_pairs={{0,1},{1,0},{2,3},{3,2},{4,5},{5,4},{6,7},{7,6},{8,9},{9,8},{10,11... | collective-permute-start | bytes 344072 | tf_op jit(solution)/shard_map/ppermute | solution.py:397
  68.8 4.4 %collective-permute-start.7 = (bf16[4,112,128]{2,1,0:T(8,128)(2,1)S(1)}, bf16[4,112,128]{2,1,0:T(8,128)(2,1)S(1)}, u32[]{:S(2)}, u32[]{:S(2)}) collective-permute-start(bf16[4,112,128]{2,1,0:T(8,128)(2,1)S(1)} %fusion.2), channel_id=1, source_target_pairs={{0,16},{16,0},{1,17},{17,1},{2,18},{18,2},{3,19},{19,3},{4,20},{20... | collective-permute-start | bytes 344072 | tf_op jit(solution)/shard_map/ppermute | solution.py:397
  73.3 3.7 %collective-permute-start.8 = (bf16[4,112,128]{2,1,0:T(8,128)(2,1)S(1)}, bf16[4,112,128]{2,1,0:T(8,128)(2,1)S(1)}, u32[]{:S(2)}, u32[]{:S(2)}) collective-permute-start(bf16[4,112,128]{2,1,0:T(8,128)(2,1)S(1)} %fusion.5), channel_id=1, source_target_pairs={{0,2},{1,3},{2,0},{3,1},{4,6},{5,7},{6,4},{7,5},{8,10},{9,11},{10,... | collective-permute-start | bytes 344072 | tf_op jit(solution)/shard_map/ppermute | solution.py:397
  77.1 3.7 %collective-permute-start.9 = (bf16[4,112,128]{2,1,0:T(8,128)(2,1)S(1)}, bf16[4,112,128]{2,1,0:T(8,128)(2,1)S(1)}, u32[]{:S(2)}, u32[]{:S(2)}) collective-permute-start(bf16[4,112,128]{2,1,0:T(8,128)(2,1)S(1)} %fusion.3), channel_id=1, source_target_pairs={{0,4},{1,5},{2,6},{3,7},{4,0},{5,1},{6,2},{7,3},{8,12},{9,13},{10,... | collective-permute-start | bytes 344072 | tf_op jit(solution)/shard_map/ppermute | solution.py:397
  80.9 5.7 %collective-permute-start.10 = (bf16[4,112,128]{2,1,0:T(8,128)(2,1)S(1)}, bf16[4,112,128]{2,1,0:T(8,128)(2,1)S(1)}, u32[]{:S(2)}, u32[]{:S(2)}) collective-permute-start(bf16[4,112,128]{2,1,0:T(8,128)(2,1)S(1)} %fusion.4), channel_id=1, source_target_pairs={{0,8},{1,9},{2,10},{3,11},{4,12},{5,13},{6,14},{7,15},{8,0},{9,1},... | collective-permute-start | bytes 344072 | tf_op jit(solution)/shard_map/ppermute | solution.py:397
  86.7 8.8 %collective-permute-start.11 = (bf16[4,112,128]{2,1,0:T(8,128)(2,1)S(1)}, bf16[4,112,128]{2,1,0:T(8,128)(2,1)S(1)}, u32[]{:S(2)}, u32[]{:S(2)}) collective-permute-start(bf16[4,112,128]{2,1,0:T(8,128)(2,1)S(1)} %get-tuple-element.21), channel_id=1, source_target_pairs={{0,1},{1,0},{2,3},{3,2},{4,5},{5,4},{6,7},{7,6},{8,9},{9,8},{10,11... | collective-permute-start | bytes 344072 | tf_op jit(solution)/shard_map/ppermute | solution.py:397
where the time goes:
time: 100 us; the launch traced here: 99.2 us
  Pallas kernels  55.4 us (55%)
  waiting for transfers between devices  19.9 us (20%)
  starting transfers between devices  15.7 us (16%)
  local copies, waits for them, and re-layouts  3.84 us (4%)
  between operations  3.21 us (3%)
  other arithmetic  1.16 us (1%)
    pallas_call x1, Pallas kernels, local(): pl.pallas_call(functools.partial(main_kernel, scale), grid_spec=pltpu.Pre...  31.9 us
    ppermute x6, waiting for transfers between devices, swap(): return lax.ppermute(values, axis, [(i, i ^ bit) for i in range(size)])  16.8 us
    pallas_call x1, Pallas kernels, local(): pl.pallas_call(functools.partial(edge_kernel, scale), grid_spec=pltpu.Pre...  12.9 us
    ppermute x6, starting transfers between devices, swap(): return lax.ppermute(values, axis, [(i, i ^ bit) for i in range(size)])  7.24 us
    pallas_call x1, Pallas kernels, local(): pl.pallas_call(functools.partial(score_kernel, channels, members_total),...  6.65 us
    ppermute x2, starting transfers between devices, exchange(): lax.ppermute(far, 'band', across)  5.17 us
    pallas_call x1, Pallas kernels, local(): pl.pallas_call(grad_kernel, grid=(members, 2), in_specs=[pl.BlockSpec((ow...  3.98 us
    ppermute x2, waiting for transfers between devices, exchange(): lax.ppermute(far, 'band', across)  3.11 us
  transfers between devices with their start and end apart: 12, of which 6 were waited for; matrix products, arithmetic and copies ran while one was open for 0% of the time, Pallas kernels for 49%

commit v1 on v0

--- a/solution.py
+++ b/solution.py
@@ -52,28 +52,54 @@
         vz[:, :, h, :, LANES:] = jnp.broadcast_to(mask.reshape(1, 1, 1, LANES), shape)
 
 
-def attend(q, kz, vz, m, p, start, offset, reach, valid):
-    rows = q.shape[0]
-    window = pl.ds(start, KEYS)
-    keys = jnp.concatenate([kz[m, p, 0, window, :], kz[m, p, 1, window, :]], axis=0)
-    values = jnp.concatenate([vz[m, p, 0, window, :], vz[m, p, 1, window, :]], axis=0)
-    logits = lax.dot_general(q, keys, NT, preferred_element_type=F32)
-    qpos = lax.broadcasted_iota(jnp.int32, (rows, KEYS), 0) + offset
-    kpos = lax.broadcasted_iota(jnp.int32, (rows, KEYS), 1)
-    away = jnp.abs(qpos - kpos)
-    if valid is not None:
-        low, high = valid
-        away = jnp.where((kpos >= low) & (kpos < high), away, 1 << 20)
-    parts = []
-    for h in range(2):
-        one = jnp.where(away <= reach[h], logits[:, h * KEYS : (h + 1) * KEYS], NEG)
-        peak = jnp.max(one, axis=1, keepdims=True)
-        parts.append(jnp.exp(one - peak).astype(BF16))
-    mixed = mm(jnp.concatenate(parts, axis=1), values)
-    return (mixed[:, :LANES] / mixed[:, LANES:]).astype(BF16)
-
-
-def main_kernel(scale, info, x, xh, wq, wk, wv, wo, dec, q_out, k_out, v_out, hid, fc, kz, vz, qs, att, res):
+def distances(offset):
+    qpos = lax.broadcasted_iota(jnp.int32, (WIN, KEYS), 0) + offset
+    return jnp.abs(qpos - lax.broadcasted_iota(jnp.int32, (WIN, KEYS), 1))
+
+
+def take(ref, *at):
+    return ref[at]
+
+
+def keep(ref, m, rows, lanes, values):
+    ref[m, rows, lanes] = values
+
+
+def attend_all(blocks, kz, vz):
+    def score(block):
+        q, m, p, start = block[:4]
+        window = pl.ds(start, KEYS)
+        keys = jnp.concatenate([kz[m, p, 0, window, :], kz[m, p, 1, window, :]], axis=0)
+        return lax.dot_general(q(), keys, NT, preferred_element_type=F32)
+
+    def soften(logits, block):
+        away, reach = block[4](), block[5]
+        parts = []
+        for h in range(2):
+            one = jnp.where(away <= reach[h], logits[:, h * KEYS : (h + 1) * KEYS], NEG)
+            peak = jnp.max(one, axis=1, keepdims=True)
+            parts.append(jnp.exp(one - peak).astype(BF16))
+        return jnp.concatenate(parts, axis=1)
+
+    def finish(probs, block):
+        m, p, start = block[1:4]
+        window = pl.ds(start, KEYS)
+        values = jnp.concatenate([vz[m, p, 0, window, :], vz[m, p, 1, window, :]], axis=0)
+        mixed = mm(probs, values)
+        block[6]((mixed[:, :LANES] / mixed[:, LANES:]).astype(BF16))
+
+    logits = score(blocks[0])
+    probs = None
+    for i, block in enumerate(blocks):
+        following = score(blocks[i + 1]) if i + 1 < len(blocks) else None
+        if probs is not None:
+            finish(probs, blocks[i - 1])
+        probs = soften(logits, block)
+        logits = following
+    finish(probs, blocks[-1])
+
+
+def main_kernel(scale, info, x, xh, wq, wk, wv, wo, dec, q_out, k_out, v_out, hid, fc, kz, vz, qs, att, res, far):
     step = pl.program_id(0)
     members, own, width = x.shape
     cols = wq.shape[1]
@@ -87,6 +113,8 @@
     @pl.when(step == 0)
     def _():
         put_ones(vz, pairs)
+        for b in range(2):
+            far[b] = distances(WIN + b * (SUB + KEYS - FRAME))
 
     flat = x[...].reshape(members * own, width)
     flat_halo = xh[...].reshape(members * HALO, width)
@@ -118,24 +146,39 @@
             put_values(vz, m, p, halo_rows, v_halo[m * HALO : (m + 1) * HALO, lanes])
 
     inner = own - 2 * WIN
+    blocks = []
     for p in range(pairs):
         reach = [info[4 + (step * pairs + p) * 2 + h] for h in range(2)]
         lanes = slice(p * LANES, (p + 1) * LANES)
         out_lanes = pl.ds(pl.multiple_of(step * cols + p * LANES, LANES), LANES)
         for m in range(members):
+
             for b in range(inner // WIN):
                 first = HALO + WIN + b * WIN
-                q = qs[m, first : first + WIN, lanes]
-                att[m, b * WIN : (b + 1) * WIN, out_lanes] = attend(
-                    q, kz, vz, m, p, first - WIN, WIN, reach, None
+                blocks.append(
+                    (
+                        functools.partial(take, qs, m, pl.ds(first, WIN), lanes),
+                        m,
+                        p,
+                        first - WIN,
+                        functools.partial(take, far, 0, slice(None), slice(None)),
+                        reach,
+                        functools.partial(keep, att, m, pl.ds(b * WIN, WIN), out_lanes),
+                    )
                 )
             for b in range(2):
-                q_rows = pl.ds(pl.multiple_of(edge + WIN + b * SUB, 16), SUB)
-                q = qs[m, q_rows, lanes]
-                start = pl.multiple_of(edge + b * (FRAME - KEYS), 32)
-                att[m, inner + b * SUB : inner + (b + 1) * SUB, out_lanes] = attend(
-                    q, kz, vz, m, p, start, WIN + b * (SUB + KEYS - FRAME), reach, None
+                blocks.append(
+                    (
+                        functools.partial(take, qs, m, pl.ds(pl.multiple_of(edge + WIN + b * SUB, 16), SUB), lanes),
+                        m,
+                        p,
+                        pl.multiple_of(edge + b * (FRAME - KEYS), 32),
+                        functools.partial(take, far, b, slice(0, SUB), slice(None)),
+                        reach,
+                        functools.partial(keep, att, m, pl.ds(inner + b * SUB, SUB), out_lanes),
+                    )
                 )
+    attend_all(blocks, kz, vz)
 
     @pl.when(step == pl.num_programs(0) - 1)
     def _():
@@ -152,7 +195,7 @@
             fc[m] = lax.dot_general(hid[m], dec[...], NT, preferred_element_type=F32)
 
 
-def edge_kernel(scale, info, x, xh, wq, wk, wv, qi, ki, vi, wo, dec, hid, fc, kz, vz, qs, att, res):
+def edge_kernel(scale, info, x, xh, wq, wk, wv, qi, ki, vi, wo, dec, hid, fc, kz, vz, qs, att, res, far):
     step = pl.program_id(0)
     members, own, width = x.shape
     cols = wq.shape[1]
@@ -167,6 +210,11 @@
     @pl.when(step == 0)
     def _():
         put_ones(vz, pairs)
+        for b in range(2):
+            start = b * (FRAME - KEYS)
+            kpos = lax.broadcasted_iota(jnp.int32, (WIN, KEYS), 1) + start
+            away = distances(WIN + b * SUB - start)
+            far[b] = jnp.where((kpos >= low) & (kpos < high), away, 1 << 20)
 
     flat_halo = xh[...].reshape(members * HALO, width)
     k_halo = mm(flat_halo, wk[...]).astype(BF16)
@@ -190,24 +238,25 @@
             put_values(vz, m, p, own_rows, vi[m, :, lanes])
             put_values(vz, m, p, halo_rows, v_halo[m * HALO : (m + 1) * HALO, lanes])
 
+    blocks = []
     for p in range(pairs):
         reach = [info[4 + (step * pairs + p) * 2 + h] for h in range(2)]
         lanes = slice(p * LANES, (p + 1) * LANES)
         out_lanes = pl.ds(pl.multiple_of(step * cols + p * LANES, LANES), LANES)
         for m in range(members):
             for b in range(2):
-                start = b * (FRAME - KEYS)
-                att[m, b * SUB : (b + 1) * SUB, out_lanes] = attend(
-                    qs[m, b * SUB : (b + 1) * SUB, lanes],
-                    kz,
-                    vz,
-                    m,
-                    p,
-                    start,
-                    WIN + b * SUB - start,
-                    reach,
-                    (low - start, high - start),
+                blocks.append(
+                    (
+                        functools.partial(take, qs, m, pl.ds(b * SUB, SUB), lanes),
+                        m,
+                        p,
+                        b * (FRAME - KEYS),
+                        functools.partial(take, far, b, slice(0, SUB), slice(None)),
+                        reach,
+                        functools.partial(keep, att, m, pl.ds(b * SUB, SUB), out_lanes),
+                    )
                 )
+    attend_all(blocks, kz, vz)
 
     @pl.when(step == pl.num_programs(0) - 1)
     def _():
@@ -368,13 +417,16 @@
             (far_own, hid_b, pl.ds(far_skip, WIN)),
         ):
             grad = grad + lax.dot_general(cot[c_rows, lanes], ref[m, h_rows, :], TN, preferred_element_type=F32)
-    keep = part.shape[1]
-    line = lax.broadcasted_iota(jnp.int32, (keep, LANES), 0)
+    chunks = width // LANES // part.shape[0]
+    extra = part.shape[1] - chunks * channels
+    line = lax.broadcasted_iota(jnp.int32, (extra, LANES), 0)
     score_high = score.astype(BF16).astype(F32)
-    extra = jnp.where(line == channels, score_high, score - score_high)
-    for chunk in range(width // LANES):
-        piece = grad[:keep, chunk * LANES : (chunk + 1) * LANES]
-        part[chunk] = jnp.where(line < channels, piece, jnp.where(line < channels + 2, extra, 0.0)).astype(BF16)
+    tail = jnp.where(line == 0, score_high, jnp.where(line == 1, score - score_high, 0.0)).astype(BF16)
+    for h in range(part.shape[0]):
+        for c in range(chunks):
+            first = (h * chunks + c) * LANES
+            part[h, c * channels : (c + 1) * channels, :] = grad[:channels, first : first + LANES].astype(BF16)
+        part[h, chunks * channels :, :] = tail
 
 
 def grad_kernel(cot, dec, out):
@@ -388,29 +440,32 @@
     return pairs
 
 
-def reduce_all(part, mesh_shape):
+def reduce_all(part, mesh_shape, beside):
     bands, count = mesh_shape["band"], mesh_shape["member"]
-    half = part.shape[0] // 2
     core = lax.axis_index("band") % 2
 
     def swap(values, axis, size, bit):
         return lax.ppermute(values, axis, [(i, i ^ bit) for i in range(size)])
 
-    mine = lax.dynamic_slice_in_dim(part, core * half, half, 0)
-    theirs = lax.dynamic_slice_in_dim(part, (1 - core) * half, half, 0)
-    total = mine.astype(F32) + swap(theirs, "band", bands, 1).astype(F32)
-    bit = 1
-    while bit < count:
-        total = total + swap(total.astype(BF16), "member", count, bit).astype(F32)
-        bit *= 2
-    bit = 2
-    while bit < bands:
-        total = total + swap(total.astype(BF16), "band", bands, bit).astype(F32)
-        bit *= 2
-    other = swap(total.astype(BF16), "band", bands, 1).astype(F32)
-    first = jnp.where(core == 0, total, other)
-    second = jnp.where(core == 0, other, total)
-    return jnp.concatenate([first, second], axis=0)
+    def add(mine, theirs):
+        return (mine.astype(F32) + theirs.astype(F32)).astype(BF16)
+
+    theirs = lax.dynamic_index_in_dim(part, 1 - core, 0, keepdims=False)
+    mine = lax.dynamic_index_in_dim(part, core, 0, keepdims=False)
+    total = add(mine, swap(theirs, "band", bands, 1))
+    steps = [("member", count, 1 << i) for i in range(count.bit_length() - 1)]
+    steps += [("band", bands, 1 << i) for i in range(1, bands.bit_length() - 1)]
+    aside = None
+    for i, (axis, size, bit) in enumerate(steps):
+        got = swap(total, axis, size, bit)
+        if i == 0:
+            aside = beside(total)
+            got, aside = lax.optimization_barrier((got, aside))
+        total = add(total, got)
+    other = swap(total, "band", bands, 1)
+    low = jnp.where(core == 0, total, other)
+    high = jnp.where(core == 0, other, total)
+    return jnp.stack([low, high]).astype(F32), aside
 
 
 def local(mesh_shape, fields, w_qkv, w_out, decoder_weight, window_reach, truth, radii):
@@ -430,7 +485,8 @@
             window_reach.astype(jnp.int32),
         ]
     )
-    inside, across = swap_pairs(bands, 0), swap_pairs(bands, 1)
+    inside = swap_pairs(bands, 0)
+    across = swap_pairs(bands, 1) + [(0, 0), (bands - 1, bands - 1)]
 
     def exchange(block, dim, size):
         last = block.shape[dim] - size
@@ -481,6 +537,7 @@
                 pltpu.VMEM((members, own + 2 * HALO, cols), BF16),
                 pltpu.VMEM((members, main_rows, width), BF16),
                 pltpu.VMEM((EDGE, width), BF16),
+                pltpu.VMEM((2, WIN, KEYS), jnp.int32),
             ],
         ),
         out_shape=[jax.ShapeDtypeStruct((members, own, width), BF16)] * 3
@@ -522,6 +579,7 @@
                 pltpu.VMEM((members, EDGE, cols), BF16),
                 pltpu.VMEM((members, EDGE, width), BF16),
                 pltpu.VMEM((members, EDGE, width), BF16),
+                pltpu.VMEM((2, WIN, KEYS), jnp.int32),
             ],
         ),
         out_shape=[
@@ -535,8 +593,8 @@
     )(info, fields, x_far, w_qkv, w_qkv, w_qkv, q_own, k_own, v_own, w_out, dec)
     other_b = lax.ppermute(fc_b, "member", member_pairs)
 
-    keep = channels + 16
-    chunks = width // LANES
+    chunks = width // LANES // 2
+    keep_rows = chunks * channels + 16
     tiles = -(-(own + 2 * RMAX) // SCORE_ROWS)
     f_rows = (tiles - 1) * SCORE_ROWS + 2 * LANES
     s_rows = own + LANES
@@ -548,7 +606,7 @@
         out_specs=[vmem, vmem],
         out_shape=[
             jax.ShapeDtypeStruct((own, members * LANES), BF16),
-            jax.ShapeDtypeStruct((chunks, keep, LANES), BF16),
+            jax.ShapeDtypeStruct((2, keep_rows, LANES), BF16),
         ],
         scratch_shapes=[
             pltpu.VMEM((f_rows, (2 * members + 1) * LANES), BF16),
@@ -559,24 +617,28 @@
         compiler_params=pltpu.CompilerParams(vmem_limit_bytes=48 * 1024 * 1024),
     )(info, radii, fc_a, fc_b, other_a, other_b, truth_t, t_near, t_far, hid_a, hid_b)
 
-    hidden_grad = pl.pallas_call(
-        grad_kernel,
-        grid=(members, 2),
-        in_specs=[
-            pl.BlockSpec((own // 2, LANES), lambda m, h: (h, m)),
-            pl.BlockSpec((LANES, width), lambda m, h: (0, 0)),
-        ],
-        out_specs=pl.BlockSpec((1, own // 2, width), lambda m, h: (m, h, 0)),
-        out_shape=jax.ShapeDtypeStruct((members, own, width), BF16),
-        cost_estimate=pl.CostEstimate(
-            flops=2 * members * own * LANES * width, bytes_accessed=3 << 20, transcendentals=0
-        ),
-    )(cot, dec)
-
-    summed = reduce_all(part, mesh_shape)
-    decoder_grad = summed[:, :channels, :].transpose(1, 0, 2).reshape(channels, width)
+    def pull_back(sent):
+        cot_now, _ = lax.optimization_barrier((cot, sent))
+        return pl.pallas_call(
+            grad_kernel,
+            grid=(members, 2),
+            in_specs=[
+                pl.BlockSpec((own // 2, LANES), lambda m, h: (h, m)),
+                pl.BlockSpec((LANES, width), lambda m, h: (0, 0)),
+            ],
+            out_specs=pl.BlockSpec((1, own // 2, width), lambda m, h: (m, h, 0)),
+            out_shape=jax.ShapeDtypeStruct((members, own, width), BF16),
+            cost_estimate=pl.CostEstimate(
+                flops=2 * members * own * LANES * width, bytes_accessed=8 << 20, transcendentals=0
+            ),
+        )(cot_now, dec)
+
+    summed, hidden_grad = reduce_all(part, mesh_shape, pull_back)
+    decoder_grad = summed[:, : chunks * channels].reshape(2 * chunks, channels, LANES)
+    decoder_grad = decoder_grad.transpose(1, 0, 2).reshape(channels, width)
     decoder_grad = decoder_grad / math.sqrt(members_total * own * bands)
-    mean_score = (summed[0, channels, 0] + summed[0, channels + 1, 0]) / (scales * channels * own * bands)
+    score = summed[0, chunks * channels, 0] + summed[0, chunks * channels + 1, 0]
+    mean_score = score / (scales * channels * own * bands)
     return (mean_score, decoder_grad, hidden_grad)
 
 

time: 100 us -> 93.5 us (0.935)
  Pallas kernels: 55.4 us -> 51.8 us
  waiting for transfers between devices: 19.9 us -> 17.2 us
  local copies, waits for them, and re-layouts: 3.84 us -> 5.54 us
    pallas_call x1, Pallas kernels: 31.9 us -> 29.1 us  [local(): pl.pallas_call(functools.partial(main_kernel, scale), grid_spec=pltpu.Pre...]
    ppermute x6, waiting for transfers between devices: 16.8 us -> 14.1 us  [swap(): return lax.ppermute(values, axis, [(i, i ^ bit) for i in range(size)])]
  transfers between devices with their start and end apart: 12 -> 12, of which waited for: 6 -> 6; matrix products, arithmetic and copies ran while one was open for 0% -> 1% of each run, Pallas kernels for 49% -> 49%
where the time goes in v1:
time: 93.5 us; the launch traced here: 93.1 us
  Pallas kernels  51.8 us (55%)
  waiting for transfers between devices  17.2 us (18%)
  starting transfers between devices  15.1 us (16%)
  local copies, waits for them, and re-layouts  5.54 us (6%)
  between operations  3.28 us (4%)
    pallas_call x1, Pallas kernels, local(): pl.pallas_call(functools.partial(main_kernel, scale), grid_spec=pltpu.Pre...  29.1 us
    ppermute x6, waiting for transfers between devices, swap(): return lax.ppermute(values, axis, [(i, i ^ bit) for i in range(size)])  14.1 us
    pallas_call x1, Pallas kernels, local(): pl.pallas_call(functools.partial(edge_kernel, scale), grid_spec=pltpu.Pre...  12.2 us
    ppermute x6, starting transfers between devices, swap(): return lax.ppermute(values, axis, [(i, i ^ bit) for i in range(size)])  6.61 us
    pallas_call x1, Pallas kernels, local(): pl.pallas_call(functools.partial(score_kernel, channels, members_total),...  6.55 us
    ppermute x2, starting transfers between devices, exchange(): lax.ppermute(far, 'band', across)  5.18 us
    pallas_call x1, Pallas kernels, pull_back(): pl.pallas_call(grad_kernel, grid=(members, 2), in_specs=[pl.BlockSpec((ow...  3.99 us
    ppermute x2, waiting for transfers between devices, exchange(): lax.ppermute(far, 'band', across)  3.1 us
  transfers between devices with their start and end apart: 12, of which 6 were waited for; matrix products, arithmetic and copies ran while one was open for 1% of the time, Pallas kernels for 49%

profile of v1, /device:TPU:25, one launch (start us, length us, event | category | flops | bytes accessed | tf_op | source)
XLA Modules:
  0.0 93.1 jit_solution(118220176554990603)
XLA Ops:
  0.7 2.3 %constant_dynamic-slice_fusion.2 = (bf16[2,160,1024]{2,1,0:T(8,128)(2,1)}, bf16[2,160,1024]{2,1,0:T(8,128)(2,1)S(1)}) fusion(bf16[2,512,1024]{2,1,0:T(8,128)(2,1)} %x.7, s32[]{:T(128)S(6)} %select_n.43, s32[]{:T(128)S(6)} %select_n.42), kind=kLoop, calls=%fused_computation.14 | loop fusion | bytes 2621448 | tf_op jit(solution)/shard_map/dynamic_slice | solution.py:494
  3.0 0.7 collective-permute-start
  3.7 3.0 %collective-permute-start.1 = (bf16[2,160,1024]{2,1,0:T(8,128)(2,1)}, bf16[2,160,1024]{2,1,0:T(8,128)(2,1)S(1)}, u32[]{:S(2)}, u32[]{:S(2)}) collective-permute-start(bf16[2,160,1024]{2,1,0:T(8,128)(2,1)} %get-tuple-element.27), channel_id=1, source_target_pairs={{1,2},{2,1},{3,4},{4,3},{5,6},{6,5},{7,8},{8,7},{9,10},{10,9},{11,... | collective-permute-start | bytes 1966088 | tf_op jit(solution)/shard_map/ppermute | solution.py:495
  6.7 0.1 concatenate.3.info
  6.8 29.1 %shard_map.94 = (bf16[2,512,1024]{2,1,0:T(8,128)(2,1)S(1)}, bf16[2,512,1024]{2,1,0:T(8,128)(2,1)}, bf16[2,512,1024]{2,1,0:T(8,128)(2,1)}, bf16[2,416,1024]{2,1,0:T(8,128)(2,1)S(1)}, f32[2,416,128]{2,1,0:T(8,128)}) custom-call(s32[20]{0:T(128)S(1)} %concatenate.3.info, bf16[2,512,1024]{2,1,0:T(8,128)(2,1)} %x.7, ...), custom_call_target="tpu_custom_call" | custom-call | flops 10737418240 | bytes 25165824 | tf_op jit(solution)/shard_map/pallas_call | solution.py:513
  35.9 1.3 %collective-permute-start.2 = (f32[2,416,128]{2,1,0:T(8,128)}, f32[2,416,128]{2,1,0:T(8,128)}, u32[]{:S(2)}, u32[]{:S(2)}) collective-permute-start(f32[2,416,128]{2,1,0:T(8,128)} %get-tuple-element.15.fa), channel_id=1, source_target_pairs={{0,16},{16,0},{1,17},{17,1},{2,18},{18,2},{3,19},{19,3},{4,20},{20... | collective-permute-start | bytes 1277960 | tf_op jit(solution)/shard_map/ppermute | solution.py:555
  37.2 0.0 collective-permute-done.1.xh
  37.2 0.0 copy-start.3
  37.3 12.2 %shard_map.95 = (bf16[2,160,1024]{2,1,0:T(8,128)(2,1)S(1)}, f32[2,160,128]{2,1,0:T(8,128)S(1)}) custom-call(s32[20]{0:T(128)S(1)} %concatenate.3.info, bf16[2,512,1024]{2,1,0:T(8,128)(2,1)S(1)} %copy-done, bf16[2,160,1024]{2,1,0:T(8,128)(2,1)S(1)} %collective-permute-done.1.xh, bf16[1024,3072]{1,0:T(8,128)(2,1)} %wv.3, bf16[1024,3072]{1,0:T(8,128)(2,1)} %wv.3, ...), custom_call_target="tpu_custom_call" | custom-call | flops 4294967296 | bytes 14680064 | tf_op jit(solution)/shard_map/pallas_call | solution.py:558
  49.4 0.3 collective-permute-start.3
  49.7 1.0 %copy.10 = f32[96,512]{0,1:T(8,128)S(1)} copy(f32[96,512]{1,0:T(8,128)} %param.12) | data formatting | bytes 393216 | tf_op args[5]
  50.8 1.1 %collective-permute-start.4 = (f32[32,128]{1,0:T(8,128)S(1)}, f32[32,128]{1,0:T(8,128)S(1)}, u32[]{:S(2)}, u32[]{:S(2)}) collective-permute-start(f32[32,128]{1,0:T(8,128)S(1)} %get-tuple-element.30), channel_id=1, source_target_pairs={{0,1},{1,0},{2,3},{3,2},{4,5},{5,4},{6,7},{7,6},{8,9},{9,8},{10,11... | collective-permute-start | bytes 49160 | tf_op jit(solution)/shard_map/ppermute | solution.py:495
  51.9 2.2 %collective-permute-start.5 = (f32[32,128]{1,0:T(8,128)S(1)}, f32[32,128]{1,0:T(8,128)S(1)}, u32[]{:S(2)}, u32[]{:S(2)}) collective-permute-start(f32[32,128]{1,0:T(8,128)S(1)} %get-tuple-element.29), channel_id=1, source_target_pairs={{1,2},{2,1},{3,4},{4,3},{5,6},{6,5},{7,8},{8,7},{9,10},{10,9},{11,... | collective-permute-start | bytes 49160 | tf_op jit(solution)/shard_map/ppermute | solution.py:495
  54.1 3.1 %collective-permute-done.5.t_far = f32[32,128]{1,0:T(8,128)S(1)} collective-permute-done((f32[32,128]{1,0:T(8,128)S(1)}, f32[32,128]{1,0:T(8,128)S(1)}, u32[]{:S(2)}, u32[]{:S(2)}) %collective-permute-start.5) | collective-permute-done | bytes 16416 | tf_op jit(solution)/shard_map/ppermute | solution.py:495
  57.2 0.0 collective-permute-done.3.gb
  57.2 6.6 %shard_map.96 = (bf16[512,256]{1,0:T(8,128)(2,1)S(1)}, bf16[2,400,128]{2,1,0:T(8,128)(2,1)S(1)}) custom-call(s32[20]{0:T(128)S(1)} %concatenate.3.info, s32[3]{0:T(128)S(1)} %copy-done.3, f32[2,416,128]{2,1,0:T(8,128)} %get-tuple-element.15.fa, f32[2,160,128]{2,1,0:T(8,128)S(1)} %get-tuple-element.19.fb, f32[2,416,128]{2,1,0:T(8,128)} %collective-permute-done.2.ga, ...), custom_call_target="tpu_custom_call" | custom-call | tf_op jit(solution)/shard_map/pallas_call | solution.py:603
  63.8 0.0 copy-start.2
  63.8 0.7 copy-done.2
  64.5 0.7 collective-permute-start.6
  65.2 0.9 %collective-permute-done.6 = bf16[400,128]{1,0:T(8,128)(2,1)S(1)} collective-permute-done((bf16[400,128]{1,0:T(8,128)(2,1)S(1)}, bf16[400,128]{1,0:T(8,128)(2,1)S(1)}, u32[]{:S(2)}, u32[]{:S(2)}) %collective-permute-start.6) | collective-permute-done | bytes 102432 | tf_op jit(solution)/shard_map/ppermute | solution.py:448
  66.2 1.3 %collective-permute-start.7 = (bf16[400,128]{1,0:T(8,128)(2,1)S(1)}, bf16[400,128]{1,0:T(8,128)(2,1)S(1)}, u32[]{:S(2)}, u32[]{:S(2)}) collective-permute-start(bf16[400,128]{1,0:T(8,128)(2,1)S(1)} %fusion), channel_id=1, source_target_pairs={{0,16},{16,0},{1,17},{17,1},{2,18},{18,2},{3,19},{19,3},{4,20},{20... | collective-permute-start | bytes 307208 | tf_op jit(solution)/shard_map/ppermute | solution.py:448
  67.5 4.0 %shard_map.97 = bf16[2,512,1024]{2,1,0:T(8,128)(2,1)} custom-call(bf16[512,256]{1,0:T(8,128)(2,1)} %copy-done.2, bf16[128,1024]{1,0:T(8,128)(2,1)} %copy-done.1), custom_call_target="tpu_custom_call" | custom-call | flops 268435456 | bytes 8388608 | tf_op jit(solution)/shard_map/pallas_call | solution.py:622
  71.5 0.1 collective-permute-start.8
  71.6 3.5 %collective-permute-done.8 = bf16[400,128]{1,0:T(8,128)(2,1)S(1)} collective-permute-done((bf16[400,128]{1,0:T(8,128)(2,1)S(1)}, bf16[400,128]{1,0:T(8,128)(2,1)S(1)}, u32[]{:S(2)}, u32[]{:S(2)}) %collective-permute-start.8) | collective-permute-done | bytes 102432 | tf_op jit(solution)/shard_map/ppermute | solution.py:448
  75.1 0.2 collective-permute-start.9
  75.4 3.3 %collective-permute-done.9 = bf16[400,128]{1,0:T(8,128)(2,1)S(1)} collective-permute-done((bf16[400,128]{1,0:T(8,128)(2,1)S(1)}, bf16[400,128]{1,0:T(8,128)(2,1)S(1)}, u32[]{:S(2)}, u32[]{:S(2)}) %collective-permute-start.9) | collective-permute-done | bytes 102432 | tf_op jit(solution)/shard_map/ppermute | solution.py:448
  78.7 0.1 collective-permute-start.10
  78.9 5.3 %collective-permute-done.10 = bf16[400,128]{1,0:T(8,128)(2,1)S(1)} collective-permute-done((bf16[400,128]{1,0:T(8,128)(2,1)S(1)}, bf16[400,128]{1,0:T(8,128)(2,1)S(1)}, u32[]{:S(2)}, u32[]{:S(2)}) %collective-permute-start.10) | collective-permute-done | bytes 102432 | tf_op jit(solution)/shard_map/ppermute | solution.py:448
  84.2 4.2 %collective-permute-start.11 = (bf16[400,128]{1,0:T(8,128)(2,1)S(1)}, bf16[400,128]{1,0:T(8,128)(2,1)S(1)}, u32[]{:S(2)}, u32[]{:S(2)}) collective-permute-start(bf16[400,128]{1,0:T(8,128)(2,1)S(1)} %add_convert_fusion), channel_id=1, source_target_pairs={{0,1},{1,0},{2,3},{3,2},{4,5},{5,4},{6,7},{7,6},{8,9},{9,8},{10,11... | collective-permute-start | bytes 307208 | tf_op jit(solution)/shard_map/ppermute | solution.py:448
  88.4 0.9 %collective-permute-done.11 = bf16[400,128]{1,0:T(8,128)(2,1)S(1)} collective-permute-done((bf16[400,128]{1,0:T(8,128)(2,1)S(1)}, bf16[400,128]{1,0:T(8,128)(2,1)S(1)}, u32[]{:S(2)}, u32[]{:S(2)}) %collective-permute-start.11) | collective-permute-done | bytes 102432 | tf_op jit(solution)/shard_map/ppermute | solution.py:448
  89.4 0.5 fusion.1
  89.9 0.8 copy.14
  (24 shorter events, 0.3 us)
Async XLA Ops:
  0.6 6.1 %copy-start.4 = (bf16[96,1024]{1,0:T(8,128)(2,1)S(1)}, bf16[96,1024]{1,0:T(8,128)(2,1)}, u32[]{:S(2)}) copy-start(bf16[96,1024]{1,0:T(8,128)(2,1)} %param.10) | copy-start | bytes 589828
  0.6 6.1 %copy-start.5 = (s32[16]{0:T(128)S(1)}, s32[16]{0:T(128)}, u32[]{:S(2)}) copy-start(s32[16]{0:T(128)} %param.11) | copy-start | bytes 196
  3.0 3.8 %collective-permute-start = (bf16[2,160,1024]{2,1,0:T(8,128)(2,1)S(1)}, bf16[2,160,1024]{2,1,0:T(8,128)(2,1)S(1)}, u32[]{:S(2)}, u32[]{:S(2)}) collective-permute-start(bf16[2,160,1024]{2,1,0:T(8,128)(2,1)S(1)} %get-tuple-element.28), channel_id=1, source_target_pairs={{0,1},{1,0},{2,3},{3,2},{4,5},{5,4},{6,7},{7,6},{8,9},{9,8},{10,11... | collective-permute-start | bytes 1966088 | tf_op jit(solution)/shard_map/ppermute | solution.py:495
  3.7 33.6 %collective-permute-start.1 = (bf16[2,160,1024]{2,1,0:T(8,128)(2,1)}, bf16[2,160,1024]{2,1,0:T(8,128)(2,1)S(1)}, u32[]{:S(2)}, u32[]{:S(2)}) collective-permute-start(bf16[2,160,1024]{2,1,0:T(8,128)(2,1)} %get-tuple-element.27), channel_id=1, source_target_pairs={{1,2},{2,1},{3,4},{4,3},{5,6},{6,5},{7,8},{8,7},{9,10},{10,9},{11,... | collective-permute-start | bytes 1966088 | tf_op jit(solution)/shard_map/ppermute | solution.py:495
  6.7 30.5 %copy-start.1 = (bf16[128,1024]{1,0:T(8,128)(2,1)}, bf16[128,1024]{1,0:T(8,128)(2,1)S(1)}, u32[]{:S(2)}) copy-start(bf16[128,1024]{1,0:T(8,128)(2,1)S(1)} %pad.8.dec) | copy-start | bytes 786436
  6.8 30.4 %copy-start = (bf16[2,512,1024]{2,1,0:T(8,128)(2,1)S(1)}, bf16[2,512,1024]{2,1,0:T(8,128)(2,1)}, u32[]{:S(2)}) copy-start(bf16[2,512,1024]{2,1,0:T(8,128)(2,1)} %x.7) | copy-start | bytes 6291460
  35.9 21.3 %collective-permute-start.2 = (f32[2,416,128]{2,1,0:T(8,128)}, f32[2,416,128]{2,1,0:T(8,128)}, u32[]{:S(2)}, u32[]{:S(2)}) collective-permute-start(f32[2,416,128]{2,1,0:T(8,128)} %get-tuple-element.15.fa), channel_id=1, source_target_pairs={{0,16},{16,0},{1,17},{17,1},{2,18},{18,2},{3,19},{19,3},{4,20},{20... | collective-permute-start | bytes 1277960 | tf_op jit(solution)/shard_map/ppermute | solution.py:555
  37.2 20.0 %copy-start.3 = (s32[3]{0:T(128)S(1)}, s32[3]{0:T(128)}, u32[]{:S(2)}) copy-start(s32[3]{0:T(128)} %radii.1) | copy-start | bytes 40
  49.4 7.8 %collective-permute-start.3 = (f32[2,160,128]{2,1,0:T(8,128)S(1)}, f32[2,160,128]{2,1,0:T(8,128)S(1)}, u32[]{:S(2)}, u32[]{:S(2)}) collective-permute-start(f32[2,160,128]{2,1,0:T(8,128)S(1)} %get-tuple-element.19.fb), channel_id=1, source_target_pairs={{0,16},{16,0},{1,17},{17,1},{2,18},{18,2},{3,19},{19,3},{4,20},{20... | collective-permute-start | bytes 491528 | tf_op jit(solution)/shard_map/ppermute | solution.py:594
  50.8 3.3 %collective-permute-start.4 = (f32[32,128]{1,0:T(8,128)S(1)}, f32[32,128]{1,0:T(8,128)S(1)}, u32[]{:S(2)}, u32[]{:S(2)}) collective-permute-start(f32[32,128]{1,0:T(8,128)S(1)} %get-tuple-element.30), channel_id=1, source_target_pairs={{0,1},{1,0},{2,3},{3,2},{4,5},{5,4},{6,7},{7,6},{8,9},{9,8},{10,11... | collective-permute-start | bytes 49160 | tf_op jit(solution)/shard_map/ppermute | solution.py:495
  51.9 5.3 %collective-permute-start.5 = (f32[32,128]{1,0:T(8,128)S(1)}, f32[32,128]{1,0:T(8,128)S(1)}, u32[]{:S(2)}, u32[]{:S(2)}) collective-permute-start(f32[32,128]{1,0:T(8,128)S(1)} %get-tuple-element.29), channel_id=1, source_target_pairs={{1,2},{2,1},{3,4},{4,3},{5,6},{6,5},{7,8},{8,7},{9,10},{10,9},{11,... | collective-permute-start | bytes 49160 | tf_op jit(solution)/shard_map/ppermute | solution.py:495
  63.8 0.7 copy-start.2
  64.5 1.7 %collective-permute-start.6 = (bf16[400,128]{1,0:T(8,128)(2,1)S(1)}, bf16[400,128]{1,0:T(8,128)(2,1)S(1)}, u32[]{:S(2)}, u32[]{:S(2)}) collective-permute-start(bf16[400,128]{1,0:T(8,128)(2,1)S(1)} %dynamic-slice_bitcast_fusion), channel_id=1, source_target_pairs={{0,1},{1,0},{2,3},{3,2},{4,5},{5,4},{6,7},{7,6},{8,9},{9,8},{10,11... | collective-permute-start | bytes 307208 | tf_op jit(solution)/shard_map/ppermute | solution.py:448
  66.2 5.3 %collective-permute-start.7 = (bf16[400,128]{1,0:T(8,128)(2,1)S(1)}, bf16[400,128]{1,0:T(8,128)(2,1)S(1)}, u32[]{:S(2)}, u32[]{:S(2)}) collective-permute-start(bf16[400,128]{1,0:T(8,128)(2,1)S(1)} %fusion), channel_id=1, source_target_pairs={{0,16},{16,0},{1,17},{17,1},{2,18},{18,2},{3,19},{19,3},{4,20},{20... | collective-permute-start | bytes 307208 | tf_op jit(solution)/shard_map/ppermute | solution.py:448
  71.5 3.6 %collective-permute-start.8 = (bf16[400,128]{1,0:T(8,128)(2,1)S(1)}, bf16[400,128]{1,0:T(8,128)(2,1)S(1)}, u32[]{:S(2)}, u32[]{:S(2)}) collective-permute-start(bf16[400,128]{1,0:T(8,128)(2,1)S(1)} %add_convert_fusion.3), channel_id=1, source_target_pairs={{0,2},{1,3},{2,0},{3,1},{4,6},{5,7},{6,4},{7,5},{8,10},{9,11},{10,... | collective-permute-start | bytes 307208 | tf_op jit(solution)/shard_map/ppermute | solution.py:448
  75.1 3.6 %collective-permute-start.9 = (bf16[400,128]{1,0:T(8,128)(2,1)S(1)}, bf16[400,128]{1,0:T(8,128)(2,1)S(1)}, u32[]{:S(2)}, u32[]{:S(2)}) collective-permute-start(bf16[400,128]{1,0:T(8,128)(2,1)S(1)} %add_convert_fusion.2), channel_id=1, source_target_pairs={{0,4},{1,5},{2,6},{3,7},{4,0},{5,1},{6,2},{7,3},{8,12},{9,13},{10,... | collective-permute-start | bytes 307208 | tf_op jit(solution)/shard_map/ppermute | solution.py:448
  78.7 5.5 %collective-permute-start.10 = (bf16[400,128]{1,0:T(8,128)(2,1)S(1)}, bf16[400,128]{1,0:T(8,128)(2,1)S(1)}, u32[]{:S(2)}, u32[]{:S(2)}) collective-permute-start(bf16[400,128]{1,0:T(8,128)(2,1)S(1)} %add_convert_fusion.1), channel_id=1, source_target_pairs={{0,8},{1,9},{2,10},{3,11},{4,12},{5,13},{6,14},{7,15},{8,0},{9,1},... | collective-permute-start | bytes 307208 | tf_op jit(solution)/shard_map/ppermute | solution.py:448
  84.2 5.1 %collective-permute-start.11 = (bf16[400,128]{1,0:T(8,128)(2,1)S(1)}, bf16[400,128]{1,0:T(8,128)(2,1)S(1)}, u32[]{:S(2)}, u32[]{:S(2)}) collective-permute-start(bf16[400,128]{1,0:T(8,128)(2,1)S(1)} %add_convert_fusion), channel_id=1, source_target_pairs={{0,1},{1,0},{2,3},{3,2},{4,5},{5,4},{6,7},{7,6},{8,9},{9,8},{10,11... | collective-permute-start | bytes 307208 | tf_op jit(solution)/shard_map/ppermute | solution.py:448

commit v2 on v1

--- a/solution.py
+++ b/solution.py
@@ -18,6 +18,7 @@
 SUB = EDGE // 2
 FRAME = EDGE + 2 * WIN
 SCORE_ROWS = 144
+CHUNK = 512
 SOFT = 0.1 * 0.1
 F32 = jnp.float32
 BF16 = jnp.bfloat16
@@ -65,7 +66,7 @@
     ref[m, rows, lanes] = values
 
 
-def attend_all(blocks, kz, vz):
+def attend_all(blocks, kz, vz, beside=()):
     def score(block):
         q, m, p, start = block[:4]
         window = pl.ds(start, KEYS)
@@ -88,10 +89,14 @@
         mixed = mm(probs, values)
         block[6]((mixed[:, :LANES] / mixed[:, LANES:]).astype(BF16))
 
+    beside = list(beside)
+    total = len(beside)
     logits = score(blocks[0])
     probs = None
     for i, block in enumerate(blocks):
         following = score(blocks[i + 1]) if i + 1 < len(blocks) else None
+        while beside and len(beside) * len(blocks) > (len(blocks) - 1 - i) * total:
+            beside.pop(0)()
         if probs is not None:
             finish(probs, blocks[i - 1])
         probs = soften(logits, block)
@@ -99,173 +104,219 @@
     finish(probs, blocks[-1])
 
 
-def main_kernel(scale, info, x, xh, wq, wk, wv, wo, dec, q_out, k_out, v_out, hid, fc, kz, vz, qs, att, res, far):
+def main_kernel(
+    scale, info, x, xh, wq, wk, wv, wo_hbm, dec, q_out, k_out, v_out, hid, fc,
+    kz0, vz0, qs0, kz1, vz1, qs1, att, res, far, wo, sem,
+):
     step = pl.program_id(0)
     members, own, width = x.shape
     cols = wq.shape[1]
     pairs = cols // LANES
-    core = info[0]
-    lower = core == 1
+    groups = width // cols
+    sets = ((kz0, vz0, qs0), (kz1, vz1, qs1))
+    lower = info[0] == 1
     halo_at = jnp.where(lower, 0, HALO + own)
     near = jnp.where(lower, WIN, 0)
     edge = jnp.where(lower, 0, own - WIN + MARGIN)
+    halo_rows = pl.ds(pl.multiple_of(halo_at, 32), HALO)
+    near_from = pl.ds(pl.multiple_of(near, 32), MARGIN)
+    near_at = pl.ds(pl.multiple_of(halo_at + near, 32), MARGIN)
+    inner = own - 2 * WIN
+    weight_copy = pltpu.make_async_copy(wo_hbm, wo, sem)
+
+    def own_chunk(kind, m, first, rows, kz, vz, qs):
+        weight = (wq, wk, wv)[kind]
+        at, to = pl.ds(first, rows), pl.ds(HALO + first, rows)
+        made = mm(x[m, at, :], weight[...]).astype(BF16)
+        if kind == 0:
+            made = (made.astype(F32) * scale).astype(BF16)
+            qs[m, to, :] = made
+        else:
+            for p in range(pairs):
+                put = (put_keys, put_values)[kind - 1]
+                put((kz, vz)[kind - 1], m, p, to, made[:, p * LANES : (p + 1) * LANES])
+        (q_out, k_out, v_out)[kind][m, at, :] = made
+
+    def halo_chunk(kind, kz, vz):
+        made = mm(xh[...].reshape(members * HALO, width), (wk, wv)[kind][...]).astype(BF16)
+        for m in range(members):
+            for p in range(pairs):
+                put = (put_keys, put_values)[kind]
+                put((kz, vz)[kind], m, p, halo_rows, made[m * HALO : (m + 1) * HALO, p * LANES : (p + 1) * LANES])
+
+    def near_chunk(qs):
+        rows = jnp.concatenate([xh[m, near_from, :] for m in range(members)], axis=0)
+        made = (mm(rows, wq[...]).astype(BF16).astype(F32) * scale).astype(BF16)
+        for m in range(members):
+            qs[m, near_at, :] = made[m * MARGIN : (m + 1) * MARGIN]
+
+    def projections(kz, vz, qs):
+        todo = []
+        for kind in (1, 2, 0):
+            for m in range(members):
+                for first in range(0, own, CHUNK):
+                    todo.append(functools.partial(own_chunk, kind, m, first, CHUNK, kz, vz, qs))
+            todo.append(functools.partial(halo_chunk, kind - 1, kz, vz) if kind else functools.partial(near_chunk, qs))
+        return todo
+
+    def attention(group, kz, vz, qs, beside=()):
+        blocks = []
+        for p in range(pairs):
+            reach = [info[4 + (group * pairs + p) * 2 + h] for h in range(2)]
+            lanes = slice(p * LANES, (p + 1) * LANES)
+            out_lanes = pl.ds(pl.multiple_of(group * cols + p * LANES, LANES), LANES)
+            for m in range(members):
+                for b in range(inner // WIN):
+                    first = HALO + WIN + b * WIN
+                    blocks.append(
+                        (
+                            functools.partial(take, qs, m, pl.ds(first, WIN), lanes),
+                            m,
+                            p,
+                            first - WIN,
+                            functools.partial(take, far, 0, slice(None), slice(None)),
+                            reach,
+                            functools.partial(keep, att, m, pl.ds(b * WIN, WIN), out_lanes),
+                        )
+                    )
+                for b in range(2):
+                    q_rows = pl.ds(pl.multiple_of(edge + WIN + b * SUB, 16), SUB)
+                    blocks.append(
+                        (
+                            functools.partial(take, qs, m, q_rows, lanes),
+                            m,
+                            p,
+                            pl.multiple_of(edge + b * (FRAME - KEYS), 32),
+                            functools.partial(take, far, b, slice(0, SUB), slice(None)),
+                            reach,
+                            functools.partial(keep, att, m, pl.ds(inner + b * SUB, SUB), out_lanes),
+                        )
+                    )
+        attend_all(blocks, kz, vz, beside)
 
     @pl.when(step == 0)
     def _():
-        put_ones(vz, pairs)
+        weight_copy.start()
+        for _, vz, _ in sets:
+            put_ones(vz, pairs)
         for b in range(2):
             far[b] = distances(WIN + b * (SUB + KEYS - FRAME))
-
-    flat = x[...].reshape(members * own, width)
-    flat_halo = xh[...].reshape(members * HALO, width)
-    k_own = mm(flat, wk[...]).astype(BF16)
-    k_halo = mm(flat_halo, wk[...]).astype(BF16)
-    v_own = mm(flat, wv[...]).astype(BF16)
-    v_halo = mm(flat_halo, wv[...]).astype(BF16)
-    q_own = mm(flat, wq[...]).astype(BF16)
-    near_rows = jnp.concatenate(
-        [xh[m, pl.ds(pl.multiple_of(near, 32), MARGIN), :] for m in range(members)], axis=0
-    )
-    q_halo = mm(near_rows, wq[...]).astype(BF16)
-    k_out[...] = k_own.reshape(members, own, cols)
-    v_out[...] = v_own.reshape(members, own, cols)
-    q_own = (q_own.astype(F32) * scale).astype(BF16)
-    q_halo = (q_halo.astype(F32) * scale).astype(BF16)
-    q_out[...] = q_own.reshape(members, own, cols)
-    own_rows = pl.ds(HALO, own)
-    halo_rows = pl.ds(pl.multiple_of(halo_at, 32), HALO)
-    q_at = pl.ds(pl.multiple_of(halo_at + near, 32), MARGIN)
-    for m in range(members):
-        qs[m, own_rows, :] = q_own[m * own : (m + 1) * own]
-        qs[m, q_at, :] = q_halo[m * MARGIN : (m + 1) * MARGIN]
-        for p in range(pairs):
-            lanes = slice(p * LANES, (p + 1) * LANES)
-            put_keys(kz, m, p, own_rows, k_own[m * own : (m + 1) * own, lanes])
-            put_keys(kz, m, p, halo_rows, k_halo[m * HALO : (m + 1) * HALO, lanes])
-            put_values(vz, m, p, own_rows, v_own[m * own : (m + 1) * own, lanes])
-            put_values(vz, m, p, halo_rows, v_halo[m * HALO : (m + 1) * HALO, lanes])
-
-    inner = own - 2 * WIN
-    blocks = []
-    for p in range(pairs):
-        reach = [info[4 + (step * pairs + p) * 2 + h] for h in range(2)]
-        lanes = slice(p * LANES, (p + 1) * LANES)
-        out_lanes = pl.ds(pl.multiple_of(step * cols + p * LANES, LANES), LANES)
-        for m in range(members):
-
-            for b in range(inner // WIN):
-                first = HALO + WIN + b * WIN
-                blocks.append(
-                    (
-                        functools.partial(take, qs, m, pl.ds(first, WIN), lanes),
-                        m,
-                        p,
-                        first - WIN,
-                        functools.partial(take, far, 0, slice(None), slice(None)),
-                        reach,
-                        functools.partial(keep, att, m, pl.ds(b * WIN, WIN), out_lanes),
-                    )
-                )
-            for b in range(2):
-                blocks.append(
-                    (
-                        functools.partial(take, qs, m, pl.ds(pl.multiple_of(edge + WIN + b * SUB, 16), SUB), lanes),
-                        m,
-                        p,
-                        pl.multiple_of(edge + b * (FRAME - KEYS), 32),
-                        functools.partial(take, far, b, slice(0, SUB), slice(None)),
-                        reach,
-                        functools.partial(keep, att, m, pl.ds(inner + b * SUB, SUB), out_lanes),
-                    )
-                )
-    attend_all(blocks, kz, vz)
-
-    @pl.when(step == pl.num_programs(0) - 1)
+        for work in projections(*sets[0]):
+            work()
+
+    for parity in range(2):
+
+        @pl.when((step > 0) & (step < groups) & (step % 2 == parity))
+        def _():
+            attention(step - 1, *sets[1 - parity], beside=projections(*sets[parity]))
+
+    @pl.when(step == groups)
     def _():
+        attention(step - 1, *sets[(groups - 1) % 2])
+        weight_copy.wait()
         own_first = jnp.where(lower, MARGIN, 0)
         from_own = pl.ds(pl.multiple_of(jnp.where(lower, 0, own - WIN), 32), WIN)
         for m in range(members):
             res[pl.ds(pl.multiple_of(own_first, 32), WIN), :] = x[m, from_own, :]
-            res[pl.ds(pl.multiple_of(jnp.where(lower, 0, WIN), 32), MARGIN), :] = xh[
-                m, pl.ds(pl.multiple_of(near, 32), MARGIN), :
-            ]
+            res[pl.ds(pl.multiple_of(jnp.where(lower, 0, WIN), 32), MARGIN), :] = xh[m, near_from, :]
             mixed = mm(att[m], wo[...])
             hid[m, :inner, :] = (mixed[:inner] + x[m, WIN : own - WIN, :].astype(F32)).astype(BF16)
             hid[m, inner:, :] = (mixed[inner:] + res[...].astype(F32)).astype(BF16)
             fc[m] = lax.dot_general(hid[m], dec[...], NT, preferred_element_type=F32)
 
 
-def edge_kernel(scale, info, x, xh, wq, wk, wv, qi, ki, vi, wo, dec, hid, fc, kz, vz, qs, att, res, far):
+def edge_kernel(
+    scale, info, x, xh, wq, wk, wv, qi, ki, vi, wo_hbm, dec, hid, fc, kz0, vz0, qs0, kz1, vz1, qs1, att, res, far, wo, sem
+):
     step = pl.program_id(0)
-    members, own, width = x.shape
+    members, _, width = x.shape
     cols = wq.shape[1]
     pairs = cols // LANES
+    groups = width // cols
+    sets = ((kz0, vz0, qs0), (kz1, vz1, qs1))
     lower = info[0] == 0
-    halo_at = jnp.where(lower, 0, 2 * WIN)
-    own_at = jnp.where(lower, HALO, 0)
-    near = jnp.where(lower, WIN, 0)
+    own_rows = pl.ds(pl.multiple_of(jnp.where(lower, HALO, 0), 32), 2 * WIN)
+    halo_rows = pl.ds(pl.multiple_of(jnp.where(lower, 0, 2 * WIN), 32), HALO)
+    near_from = pl.ds(pl.multiple_of(jnp.where(lower, WIN, 0), 32), MARGIN)
+    own_at = pl.ds(pl.multiple_of(jnp.where(lower, MARGIN, 0), 32), WIN)
+    near_at = pl.ds(pl.multiple_of(jnp.where(lower, 0, WIN), 32), MARGIN)
     low = jnp.where(info[1] == 1, HALO, 0)
     high = jnp.where(info[2] == 1, 2 * WIN, FRAME)
+    weight_copy = pltpu.make_async_copy(wo_hbm, wo, sem)
+
+    def own_chunk(kind, m, p, target):
+        lanes = slice(p * LANES, (p + 1) * LANES)
+        (put_keys, put_values)[kind](target, m, p, own_rows, (ki, vi)[kind][m, :, lanes])
+
+    def halo_chunk(kind, m, kz, vz):
+        made = mm(xh[m], (wk, wv)[kind][...]).astype(BF16)
+        for p in range(pairs):
+            (put_keys, put_values)[kind]((kz, vz)[kind], m, p, halo_rows, made[:, p * LANES : (p + 1) * LANES])
+
+    def query_chunk(qs):
+        rows = jnp.concatenate([xh[m, near_from, :] for m in range(members)], axis=0)
+        made = (mm(rows, wq[...]).astype(BF16).astype(F32) * scale).astype(BF16)
+        for m in range(members):
+            qs[m, own_at, :] = qi[m]
+            qs[m, near_at, :] = made[m * MARGIN : (m + 1) * MARGIN]
+
+    def projections(kz, vz, qs):
+        todo = []
+        for kind in range(2):
+            for m in range(members):
+                todo.append(functools.partial(halo_chunk, kind, m, kz, vz))
+                for p in range(pairs):
+                    todo.append(functools.partial(own_chunk, kind, m, p, (kz, vz)[kind]))
+        todo.append(functools.partial(query_chunk, qs))
+        return todo
+
+    def attention(group, kz, vz, qs, beside=()):
+        blocks = []
+        for p in range(pairs):
+            reach = [info[4 + (group * pairs + p) * 2 + h] for h in range(2)]
+            lanes = slice(p * LANES, (p + 1) * LANES)
+            out_lanes = pl.ds(pl.multiple_of(group * cols + p * LANES, LANES), LANES)
+            for m in range(members):
+                for b in range(2):
+                    blocks.append(
+                        (
+                            functools.partial(take, qs, m, pl.ds(b * SUB, SUB), lanes),
+                            m,
+                            p,
+                            b * (FRAME - KEYS),
+                            functools.partial(take, far, b, slice(0, SUB), slice(None)),
+                            reach,
+                            functools.partial(keep, att, m, pl.ds(b * SUB, SUB), out_lanes),
+                        )
+                    )
+        attend_all(blocks, kz, vz, beside)
 
     @pl.when(step == 0)
     def _():
-        put_ones(vz, pairs)
+        weight_copy.start()
+        for _, vz, _ in sets:
+            put_ones(vz, pairs)
         for b in range(2):
             start = b * (FRAME - KEYS)
             kpos = lax.broadcasted_iota(jnp.int32, (WIN, KEYS), 1) + start
             away = distances(WIN + b * SUB - start)
             far[b] = jnp.where((kpos >= low) & (kpos < high), away, 1 << 20)
-
-    flat_halo = xh[...].reshape(members * HALO, width)
-    k_halo = mm(flat_halo, wk[...]).astype(BF16)
-    v_halo = mm(flat_halo, wv[...]).astype(BF16)
-    near_rows = jnp.concatenate(
-        [xh[m, pl.ds(pl.multiple_of(near, 32), MARGIN), :] for m in range(members)], axis=0
-    )
-    q_halo = mm(near_rows, wq[...]).astype(BF16)
-    q_halo = (q_halo.astype(F32) * scale).astype(BF16)
-    own_rows = pl.ds(pl.multiple_of(own_at, 32), 2 * WIN)
-    halo_rows = pl.ds(pl.multiple_of(halo_at, 32), HALO)
-    for m in range(members):
-        qs[m, pl.ds(pl.multiple_of(jnp.where(lower, MARGIN, 0), 32), WIN), :] = qi[m]
-        qs[m, pl.ds(pl.multiple_of(jnp.where(lower, 0, WIN), 32), MARGIN), :] = q_halo[
-            m * MARGIN : (m + 1) * MARGIN
-        ]
-        for p in range(pairs):
-            lanes = slice(p * LANES, (p + 1) * LANES)
-            put_keys(kz, m, p, own_rows, ki[m, :, lanes])
-            put_keys(kz, m, p, halo_rows, k_halo[m * HALO : (m + 1) * HALO, lanes])
-            put_values(vz, m, p, own_rows, vi[m, :, lanes])
-            put_values(vz, m, p, halo_rows, v_halo[m * HALO : (m + 1) * HALO, lanes])
-
-    blocks = []
-    for p in range(pairs):
-        reach = [info[4 + (step * pairs + p) * 2 + h] for h in range(2)]
-        lanes = slice(p * LANES, (p + 1) * LANES)
-        out_lanes = pl.ds(pl.multiple_of(step * cols + p * LANES, LANES), LANES)
+        for work in projections(*sets[0]):
+            work()
+
+    for parity in range(2):
+
+        @pl.when((step > 0) & (step < groups) & (step % 2 == parity))
+        def _():
+            attention(step - 1, *sets[1 - parity], beside=projections(*sets[parity]))
+
+    @pl.when(step == groups)
+    def _():
+        attention(step - 1, *sets[(groups - 1) % 2])
+        weight_copy.wait()
         for m in range(members):
-            for b in range(2):
-                blocks.append(
-                    (
-                        functools.partial(take, qs, m, pl.ds(b * SUB, SUB), lanes),
-                        m,
-                        p,
-                        b * (FRAME - KEYS),
-                        functools.partial(take, far, b, slice(0, SUB), slice(None)),
-                        reach,
-                        functools.partial(keep, att, m, pl.ds(b * SUB, SUB), out_lanes),
-                    )
-                )
-    attend_all(blocks, kz, vz)
-
-    @pl.when(step == pl.num_programs(0) - 1)
-    def _():
-        from_own = pl.ds(pl.multiple_of(jnp.where(lower, 0, own - WIN), 32), WIN)
-        for m in range(members):
-            res[m, pl.ds(pl.multiple_of(jnp.where(lower, MARGIN, 0), 32), WIN), :] = x[m, from_own, :]
-            res[m, pl.ds(pl.multiple_of(jnp.where(lower, 0, WIN), 32), MARGIN), :] = xh[
-                m, pl.ds(pl.multiple_of(near, 32), MARGIN), :
-            ]
+            res[m, own_at, :] = x[m]
+            res[m, near_at, :] = xh[m, near_from, :]
         mixed = mm(att[...].reshape(members * EDGE, width), wo[...])
         hidden = (mixed + res[...].reshape(members * EDGE, width).astype(F32)).astype(BF16)
         hid[...] = hidden.reshape(members, EDGE, width)
@@ -503,41 +554,49 @@
     steps = width // cols
     pairs = cols // LANES
     whole = lambda shape: pl.BlockSpec(shape, lambda i, s: (0,) * len(shape))
-    weight = lambda third: pl.BlockSpec((width, cols), lambda i, s: (0, third * steps + i))
     inner = own - 2 * WIN
     main_rows = inner + EDGE
     col_block = lambda rows: pl.BlockSpec((members, rows, cols), lambda i, s: (0, 0, i))
     params = pltpu.CompilerParams(
         dimension_semantics=("arbitrary",), vmem_limit_bytes=48 * 1024 * 1024
     )
+    group_block = lambda rows: pl.BlockSpec((members, rows, cols), lambda i, s: (0, 0, jnp.minimum(i, steps - 1)))
+    group_weight = lambda third: pl.BlockSpec(
+        (width, cols), lambda i, s: (0, third * steps + jnp.minimum(i, steps - 1))
+    )
+    work_set = [
+        pltpu.VMEM((members, pairs, 2, own + 2 * HALO, LANES), BF16),
+        pltpu.VMEM((members, pairs, 2, own + 2 * HALO, 2 * LANES), BF16),
+        pltpu.VMEM((members, own + 2 * HALO, cols), BF16),
+    ]
     q_own, k_own, v_own, hid_a, fc_a = pl.pallas_call(
         functools.partial(main_kernel, scale),
         grid_spec=pltpu.PrefetchScalarGridSpec(
             num_scalar_prefetch=1,
-            grid=(steps,),
+            grid=(steps + 1,),
             in_specs=[
                 whole((members, own, width)),
                 whole((members, HALO, width)),
-                weight(0),
-                weight(1),
-                weight(2),
-                whole((width, width)),
+                group_weight(0),
+                group_weight(1),
+                group_weight(2),
+                pl.BlockSpec(memory_space=pl.ANY),
                 whole((LANES, width)),
             ],
             out_specs=[
-                col_block(own),
-                col_block(own),
-                col_block(own),
+                group_block(own),
+                group_block(own),
+                group_block(own),
                 whole((members, main_rows, width)),
                 whole((members, main_rows, LANES)),
             ],
-            scratch_shapes=[
-                pltpu.VMEM((members, pairs, 2, own + 2 * HALO, LANES), BF16),
-                pltpu.VMEM((members, pairs, 2, own + 2 * HALO, 2 * LANES), BF16),
-                pltpu.VMEM((members, own + 2 * HALO, cols), BF16),
+            scratch_shapes=work_set * 2
+            + [
                 pltpu.VMEM((members, main_rows, width), BF16),
                 pltpu.VMEM((EDGE, width), BF16),
                 pltpu.VMEM((2, WIN, KEYS), jnp.int32),
+                pltpu.VMEM((width, width), BF16),
+                pltpu.SemaphoreType.DMA,
             ],
         ),
         out_shape=[jax.ShapeDtypeStruct((members, own, width), BF16)] * 3
@@ -554,22 +613,24 @@
     member_pairs = [(i, i ^ 1) for i in range(member_count)]
     other_a = lax.ppermute(fc_a, "member", member_pairs)
 
-    far_block = lambda rows, last: pl.BlockSpec((members, rows, cols), lambda i, s: (0, s[0] * last, i))
+    far_block = lambda rows, last: pl.BlockSpec(
+        (members, rows, cols), lambda i, s: (0, s[0] * last, jnp.minimum(i, steps - 1))
+    )
     hid_b, fc_b = pl.pallas_call(
         functools.partial(edge_kernel, scale),
         grid_spec=pltpu.PrefetchScalarGridSpec(
             num_scalar_prefetch=1,
-            grid=(steps,),
+            grid=(steps + 1,),
             in_specs=[
-                whole((members, own, width)),
+                pl.BlockSpec((members, WIN, width), lambda i, s: (0, s[0] * (own // WIN - 1), 0)),
                 whole((members, HALO, width)),
-                weight(0),
-                weight(1),
-                weight(2),
+                group_weight(0),
+                group_weight(1),
+                group_weight(2),
                 far_block(WIN, own // WIN - 1),
                 far_block(2 * WIN, own // (2 * WIN) - 1),
                 far_block(2 * WIN, own // (2 * WIN) - 1),
-                whole((width, width)),
+                pl.BlockSpec(memory_space=pl.ANY),
                 whole((LANES, width)),
             ],
             out_specs=[whole((members, EDGE, width)), whole((members, EDGE, LANES))],
@@ -577,9 +638,14 @@
                 pltpu.VMEM((members, pairs, 2, FRAME, LANES), BF16),
                 pltpu.VMEM((members, pairs, 2, FRAME, 2 * LANES), BF16),
                 pltpu.VMEM((members, EDGE, cols), BF16),
+            ]
+            * 2
+            + [
                 pltpu.VMEM((members, EDGE, width), BF16),
                 pltpu.VMEM((members, EDGE, width), BF16),
                 pltpu.VMEM((2, WIN, KEYS), jnp.int32),
+                pltpu.VMEM((width, width), BF16),
+                pltpu.SemaphoreType.DMA,
             ],
         ),
         out_shape=[

time: 93.5 us -> 88 us (0.941)
  Pallas kernels: 51.8 us -> 46.3 us
    pallas_call x1, Pallas kernels: 29.1 us -> 24.6 us  [local(): pl.pallas_call(functools.partial(main_kernel, scale), grid_spec=pltpu.Pre...]
  transfers between devices with their start and end apart: 12 -> 12, of which waited for: 6 -> 6; matrix products, arithmetic and copies ran while one was open for 1% -> 1% of each run, Pallas kernels for 49% -> 46%
where the time goes in v2:
time: 88 us; the launch traced here: 87.6 us
  Pallas kernels  46.3 us (53%)
  waiting for transfers between devices  17.2 us (20%)
  starting transfers between devices  15.1 us (17%)
  local copies, waits for them, and re-layouts  5.54 us (6%)
  between operations  3.28 us (4%)
    pallas_call x1, Pallas kernels, local(): pl.pallas_call(functools.partial(main_kernel, scale), grid_spec=pltpu.Pre...  24.6 us
    ppermute x6, waiting for transfers between devices, swap(): return lax.ppermute(values, axis, [(i, i ^ bit) for i in range(size)])  14.1 us
    pallas_call x1, Pallas kernels, local(): pl.pallas_call(functools.partial(edge_kernel, scale), grid_spec=pltpu.Pre...  11.3 us
    ppermute x6, starting transfers between devices, swap(): return lax.ppermute(values, axis, [(i, i ^ bit) for i in range(size)])  6.59 us
    pallas_call x1, Pallas kernels, local(): pl.pallas_call(functools.partial(score_kernel, channels, members_total),...  6.39 us
    ppermute x2, starting transfers between devices, exchange(): lax.ppermute(far, 'band', across)  5.19 us
    pallas_call x1, Pallas kernels, pull_back(): pl.pallas_call(grad_kernel, grid=(members, 2), in_specs=[pl.BlockSpec((ow...  3.99 us
    ppermute x2, waiting for transfers between devices, exchange(): lax.ppermute(far, 'band', across)  3.09 us
  transfers between devices with their start and end apart: 12, of which 6 were waited for; matrix products, arithmetic and copies ran while one was open for 1% of the time, Pallas kernels for 46%

profile of v2, /device:TPU:25, one launch (start us, length us, event | category | flops | bytes accessed | tf_op | source)
XLA Modules:
  0.0 87.6 jit_solution(3566460438955894246)
XLA Ops:
  0.7 2.3 %constant_dynamic-slice_fusion.2 = (bf16[2,160,1024]{2,1,0:T(8,128)(2,1)}, bf16[2,160,1024]{2,1,0:T(8,128)(2,1)S(1)}) fusion(bf16[2,512,1024]{2,1,0:T(8,128)(2,1)} %x.7, s32[]{:T(128)S(6)} %select_n.43, s32[]{:T(128)S(6)} %select_n.42), kind=kLoop, calls=%fused_computation.14 | loop fusion | bytes 2621448 | tf_op jit(solution)/shard_map/dynamic_slice | solution.py:545
  3.0 0.7 collective-permute-start
  3.7 3.0 %collective-permute-start.1 = (bf16[2,160,1024]{2,1,0:T(8,128)(2,1)}, bf16[2,160,1024]{2,1,0:T(8,128)(2,1)S(1)}, u32[]{:S(2)}, u32[]{:S(2)}) collective-permute-start(bf16[2,160,1024]{2,1,0:T(8,128)(2,1)} %get-tuple-element.27), channel_id=1, source_target_pairs={{1,2},{2,1},{3,4},{4,3},{5,6},{6,5},{7,8},{8,7},{9,10},{10,9},{11,... | collective-permute-start | bytes 1966088 | tf_op jit(solution)/shard_map/ppermute | solution.py:546
  6.7 0.1 concatenate.3.info
  6.8 24.6 %shard_map.94 = (bf16[2,512,1024]{2,1,0:T(8,128)(2,1)S(1)}, bf16[2,512,1024]{2,1,0:T(8,128)(2,1)}, bf16[2,512,1024]{2,1,0:T(8,128)(2,1)}, bf16[2,416,1024]{2,1,0:T(8,128)(2,1)S(1)}, f32[2,416,128]{2,1,0:T(8,128)}) custom-call(s32[20]{0:T(128)S(1)} %concatenate.3.info, bf16[2,512,1024]{2,1,0:T(8,128)(2,1)} %x.7, ...), custom_call_target="tpu_custom_call" | custom-call | flops 10737418240 | bytes 25165824 | tf_op jit(solution)/shard_map/pallas_call | solution.py:572
  31.4 1.3 %collective-permute-start.2 = (f32[2,416,128]{2,1,0:T(8,128)}, f32[2,416,128]{2,1,0:T(8,128)}, u32[]{:S(2)}, u32[]{:S(2)}) collective-permute-start(f32[2,416,128]{2,1,0:T(8,128)} %get-tuple-element.15.fa), channel_id=1, source_target_pairs={{0,16},{16,0},{1,17},{17,1},{2,18},{18,2},{3,19},{19,3},{4,20},{20... | collective-permute-start | bytes 1277960 | tf_op jit(solution)/shard_map/ppermute | solution.py:614
  32.7 0.0 copy-start.3
  32.7 11.3 %shard_map.95 = (bf16[2,160,1024]{2,1,0:T(8,128)(2,1)S(1)}, f32[2,160,128]{2,1,0:T(8,128)S(1)}) custom-call(s32[20]{0:T(128)S(1)} %concatenate.3.info, bf16[2,512,1024]{2,1,0:T(8,128)(2,1)S(1)} %copy-done, bf16[2,160,1024]{2,1,0:T(8,128)(2,1)S(1)} %collective-permute-done.1.xh, bf16[1024,3072]{1,0:T(8,128)(2,1)} %wv.3, bf16[1024,3072]{1,0:T(8,128)(2,1)} %wv.3, ...), custom_call_target="tpu_custom_call" | custom-call | flops 4294967296 | bytes 14680064 | tf_op jit(solution)/shard_map/pallas_call | solution.py:619
  44.1 0.3 collective-permute-start.3
  44.4 1.0 %copy.10 = f32[96,512]{0,1:T(8,128)S(1)} copy(f32[96,512]{1,0:T(8,128)} %param.12) | data formatting | bytes 393216 | tf_op args[5]
  45.5 1.0 %collective-permute-start.4 = (f32[32,128]{1,0:T(8,128)S(1)}, f32[32,128]{1,0:T(8,128)S(1)}, u32[]{:S(2)}, u32[]{:S(2)}) collective-permute-start(f32[32,128]{1,0:T(8,128)S(1)} %get-tuple-element.30), channel_id=1, source_target_pairs={{0,1},{1,0},{2,3},{3,2},{4,5},{5,4},{6,7},{7,6},{8,9},{9,8},{10,11... | collective-permute-start | bytes 49160 | tf_op jit(solution)/shard_map/ppermute | solution.py:546
  46.5 2.2 %collective-permute-start.5 = (f32[32,128]{1,0:T(8,128)S(1)}, f32[32,128]{1,0:T(8,128)S(1)}, u32[]{:S(2)}, u32[]{:S(2)}) collective-permute-start(f32[32,128]{1,0:T(8,128)S(1)} %get-tuple-element.29), channel_id=1, source_target_pairs={{1,2},{2,1},{3,4},{4,3},{5,6},{6,5},{7,8},{8,7},{9,10},{10,9},{11,... | collective-permute-start | bytes 49160 | tf_op jit(solution)/shard_map/ppermute | solution.py:546
  48.8 0.0 collective-permute-done.4.t_near
  48.8 3.1 %collective-permute-done.5.t_far = f32[32,128]{1,0:T(8,128)S(1)} collective-permute-done((f32[32,128]{1,0:T(8,128)S(1)}, f32[32,128]{1,0:T(8,128)S(1)}, u32[]{:S(2)}, u32[]{:S(2)}) %collective-permute-start.5) | collective-permute-done | bytes 16416 | tf_op jit(solution)/shard_map/ppermute | solution.py:546
  51.9 0.0 collective-permute-done.3.gb
  51.9 6.4 %shard_map.96 = (bf16[512,256]{1,0:T(8,128)(2,1)S(1)}, bf16[2,400,128]{2,1,0:T(8,128)(2,1)S(1)}) custom-call(s32[20]{0:T(128)S(1)} %concatenate.3.info, s32[3]{0:T(128)S(1)} %copy-done.3, f32[2,416,128]{2,1,0:T(8,128)} %get-tuple-element.15.fa, f32[2,160,128]{2,1,0:T(8,128)S(1)} %get-tuple-element.19.fb, f32[2,416,128]{2,1,0:T(8,128)} %collective-permute-done.2.ga, ...), custom_call_target="tpu_custom_call" | custom-call | tf_op jit(solution)/shard_map/pallas_call | solution.py:669
  58.3 0.0 copy-start.2
  58.3 0.7 copy-done.2
  59.0 0.7 collective-permute-start.6
  59.7 0.9 %collective-permute-done.6 = bf16[400,128]{1,0:T(8,128)(2,1)S(1)} collective-permute-done((bf16[400,128]{1,0:T(8,128)(2,1)S(1)}, bf16[400,128]{1,0:T(8,128)(2,1)S(1)}, u32[]{:S(2)}, u32[]{:S(2)}) %collective-permute-start.6) | collective-permute-done | bytes 102432 | tf_op jit(solution)/shard_map/ppermute | solution.py:499
  60.7 1.3 %collective-permute-start.7 = (bf16[400,128]{1,0:T(8,128)(2,1)S(1)}, bf16[400,128]{1,0:T(8,128)(2,1)S(1)}, u32[]{:S(2)}, u32[]{:S(2)}) collective-permute-start(bf16[400,128]{1,0:T(8,128)(2,1)S(1)} %fusion), channel_id=1, source_target_pairs={{0,16},{16,0},{1,17},{17,1},{2,18},{18,2},{3,19},{19,3},{4,20},{20... | collective-permute-start | bytes 307208 | tf_op jit(solution)/shard_map/ppermute | solution.py:499
  62.0 4.0 %shard_map.97 = bf16[2,512,1024]{2,1,0:T(8,128)(2,1)} custom-call(bf16[512,256]{1,0:T(8,128)(2,1)} %copy-done.2, bf16[128,1024]{1,0:T(8,128)(2,1)} %copy-done.1), custom_call_target="tpu_custom_call" | custom-call | flops 268435456 | bytes 8388608 | tf_op jit(solution)/shard_map/pallas_call | solution.py:688
  66.0 0.1 collective-permute-start.8
  66.1 3.5 %collective-permute-done.8 = bf16[400,128]{1,0:T(8,128)(2,1)S(1)} collective-permute-done((bf16[400,128]{1,0:T(8,128)(2,1)S(1)}, bf16[400,128]{1,0:T(8,128)(2,1)S(1)}, u32[]{:S(2)}, u32[]{:S(2)}) %collective-permute-start.8) | collective-permute-done | bytes 102432 | tf_op jit(solution)/shard_map/ppermute | solution.py:499
  69.6 0.2 collective-permute-start.9
  69.8 3.3 %collective-permute-done.9 = bf16[400,128]{1,0:T(8,128)(2,1)S(1)} collective-permute-done((bf16[400,128]{1,0:T(8,128)(2,1)S(1)}, bf16[400,128]{1,0:T(8,128)(2,1)S(1)}, u32[]{:S(2)}, u32[]{:S(2)}) %collective-permute-start.9) | collective-permute-done | bytes 102432 | tf_op jit(solution)/shard_map/ppermute | solution.py:499
  73.2 0.1 collective-permute-start.10
  73.4 5.3 %collective-permute-done.10 = bf16[400,128]{1,0:T(8,128)(2,1)S(1)} collective-permute-done((bf16[400,128]{1,0:T(8,128)(2,1)S(1)}, bf16[400,128]{1,0:T(8,128)(2,1)S(1)}, u32[]{:S(2)}, u32[]{:S(2)}) %collective-permute-start.10) | collective-permute-done | bytes 102432 | tf_op jit(solution)/shard_map/ppermute | solution.py:499
  78.7 4.2 %collective-permute-start.11 = (bf16[400,128]{1,0:T(8,128)(2,1)S(1)}, bf16[400,128]{1,0:T(8,128)(2,1)S(1)}, u32[]{:S(2)}, u32[]{:S(2)}) collective-permute-start(bf16[400,128]{1,0:T(8,128)(2,1)S(1)} %add_convert_fusion), channel_id=1, source_target_pairs={{0,1},{1,0},{2,3},{3,2},{4,5},{5,4},{6,7},{7,6},{8,9},{9,8},{10,11... | collective-permute-start | bytes 307208 | tf_op jit(solution)/shard_map/ppermute | solution.py:499
  82.9 0.9 %collective-permute-done.11 = bf16[400,128]{1,0:T(8,128)(2,1)S(1)} collective-permute-done((bf16[400,128]{1,0:T(8,128)(2,1)S(1)}, bf16[400,128]{1,0:T(8,128)(2,1)S(1)}, u32[]{:S(2)}, u32[]{:S(2)}) %collective-permute-start.11) | collective-permute-done | bytes 102432 | tf_op jit(solution)/shard_map/ppermute | solution.py:499
  83.8 0.5 fusion.1
  84.4 0.8 copy.14
  (24 shorter events, 0.3 us)
Async XLA Ops:
  0.6 6.1 %copy-start.4 = (bf16[96,1024]{1,0:T(8,128)(2,1)S(1)}, bf16[96,1024]{1,0:T(8,128)(2,1)}, u32[]{:S(2)}) copy-start(bf16[96,1024]{1,0:T(8,128)(2,1)} %param.10) | copy-start | bytes 589828
  0.6 6.1 %copy-start.5 = (s32[16]{0:T(128)S(1)}, s32[16]{0:T(128)}, u32[]{:S(2)}) copy-start(s32[16]{0:T(128)} %param.11) | copy-start | bytes 196
  3.0 3.8 %collective-permute-start = (bf16[2,160,1024]{2,1,0:T(8,128)(2,1)S(1)}, bf16[2,160,1024]{2,1,0:T(8,128)(2,1)S(1)}, u32[]{:S(2)}, u32[]{:S(2)}) collective-permute-start(bf16[2,160,1024]{2,1,0:T(8,128)(2,1)S(1)} %get-tuple-element.28), channel_id=1, source_target_pairs={{0,1},{1,0},{2,3},{3,2},{4,5},{5,4},{6,7},{7,6},{8,9},{9,8},{10,11... | collective-permute-start | bytes 1966088 | tf_op jit(solution)/shard_map/ppermute | solution.py:546
  3.7 29.0 %collective-permute-start.1 = (bf16[2,160,1024]{2,1,0:T(8,128)(2,1)}, bf16[2,160,1024]{2,1,0:T(8,128)(2,1)S(1)}, u32[]{:S(2)}, u32[]{:S(2)}) collective-permute-start(bf16[2,160,1024]{2,1,0:T(8,128)(2,1)} %get-tuple-element.27), channel_id=1, source_target_pairs={{1,2},{2,1},{3,4},{4,3},{5,6},{6,5},{7,8},{8,7},{9,10},{10,9},{11,... | collective-permute-start | bytes 1966088 | tf_op jit(solution)/shard_map/ppermute | solution.py:546
  6.7 26.0 %copy-start.1 = (bf16[128,1024]{1,0:T(8,128)(2,1)}, bf16[128,1024]{1,0:T(8,128)(2,1)S(1)}, u32[]{:S(2)}) copy-start(bf16[128,1024]{1,0:T(8,128)(2,1)S(1)} %pad.8.dec) | copy-start | bytes 786436
  6.8 25.9 %copy-start = (bf16[2,512,1024]{2,1,0:T(8,128)(2,1)S(1)}, bf16[2,512,1024]{2,1,0:T(8,128)(2,1)}, u32[]{:S(2)}) copy-start(bf16[2,512,1024]{2,1,0:T(8,128)(2,1)} %x.7) | copy-start | bytes 6291460
  31.4 20.5 %collective-permute-start.2 = (f32[2,416,128]{2,1,0:T(8,128)}, f32[2,416,128]{2,1,0:T(8,128)}, u32[]{:S(2)}, u32[]{:S(2)}) collective-permute-start(f32[2,416,128]{2,1,0:T(8,128)} %get-tuple-element.15.fa), channel_id=1, source_target_pairs={{0,16},{16,0},{1,17},{17,1},{2,18},{18,2},{3,19},{19,3},{4,20},{20... | collective-permute-start | bytes 1277960 | tf_op jit(solution)/shard_map/ppermute | solution.py:614
  32.7 19.2 %copy-start.3 = (s32[3]{0:T(128)S(1)}, s32[3]{0:T(128)}, u32[]{:S(2)}) copy-start(s32[3]{0:T(128)} %radii.1) | copy-start | bytes 40
  44.1 7.8 %collective-permute-start.3 = (f32[2,160,128]{2,1,0:T(8,128)S(1)}, f32[2,160,128]{2,1,0:T(8,128)S(1)}, u32[]{:S(2)}, u32[]{:S(2)}) collective-permute-start(f32[2,160,128]{2,1,0:T(8,128)S(1)} %get-tuple-element.19.fb), channel_id=1, source_target_pairs={{0,16},{16,0},{1,17},{17,1},{2,18},{18,2},{3,19},{19,3},{4,20},{20... | collective-permute-start | bytes 491528 | tf_op jit(solution)/shard_map/ppermute | solution.py:660
  45.5 3.3 %collective-permute-start.4 = (f32[32,128]{1,0:T(8,128)S(1)}, f32[32,128]{1,0:T(8,128)S(1)}, u32[]{:S(2)}, u32[]{:S(2)}) collective-permute-start(f32[32,128]{1,0:T(8,128)S(1)} %get-tuple-element.30), channel_id=1, source_target_pairs={{0,1},{1,0},{2,3},{3,2},{4,5},{5,4},{6,7},{7,6},{8,9},{9,8},{10,11... | collective-permute-start | bytes 49160 | tf_op jit(solution)/shard_map/ppermute | solution.py:546
  46.5 5.3 %collective-permute-start.5 = (f32[32,128]{1,0:T(8,128)S(1)}, f32[32,128]{1,0:T(8,128)S(1)}, u32[]{:S(2)}, u32[]{:S(2)}) collective-permute-start(f32[32,128]{1,0:T(8,128)S(1)} %get-tuple-element.29), channel_id=1, source_target_pairs={{1,2},{2,1},{3,4},{4,3},{5,6},{6,5},{7,8},{8,7},{9,10},{10,9},{11,... | collective-permute-start | bytes 49160 | tf_op jit(solution)/shard_map/ppermute | solution.py:546
  58.3 0.7 copy-start.2
  59.0 1.6 %collective-permute-start.6 = (bf16[400,128]{1,0:T(8,128)(2,1)S(1)}, bf16[400,128]{1,0:T(8,128)(2,1)S(1)}, u32[]{:S(2)}, u32[]{:S(2)}) collective-permute-start(bf16[400,128]{1,0:T(8,128)(2,1)S(1)} %dynamic-slice_bitcast_fusion), channel_id=1, source_target_pairs={{0,1},{1,0},{2,3},{3,2},{4,5},{5,4},{6,7},{7,6},{8,9},{9,8},{10,11... | collective-permute-start | bytes 307208 | tf_op jit(solution)/shard_map/ppermute | solution.py:499
  60.7 5.3 %collective-permute-start.7 = (bf16[400,128]{1,0:T(8,128)(2,1)S(1)}, bf16[400,128]{1,0:T(8,128)(2,1)S(1)}, u32[]{:S(2)}, u32[]{:S(2)}) collective-permute-start(bf16[400,128]{1,0:T(8,128)(2,1)S(1)} %fusion), channel_id=1, source_target_pairs={{0,16},{16,0},{1,17},{17,1},{2,18},{18,2},{3,19},{19,3},{4,20},{20... | collective-permute-start | bytes 307208 | tf_op jit(solution)/shard_map/ppermute | solution.py:499
  66.0 3.6 %collective-permute-start.8 = (bf16[400,128]{1,0:T(8,128)(2,1)S(1)}, bf16[400,128]{1,0:T(8,128)(2,1)S(1)}, u32[]{:S(2)}, u32[]{:S(2)}) collective-permute-start(bf16[400,128]{1,0:T(8,128)(2,1)S(1)} %add_convert_fusion.3), channel_id=1, source_target_pairs={{0,2},{1,3},{2,0},{3,1},{4,6},{5,7},{6,4},{7,5},{8,10},{9,11},{10,... | collective-permute-start | bytes 307208 | tf_op jit(solution)/shard_map/ppermute | solution.py:499
  69.6 3.6 %collective-permute-start.9 = (bf16[400,128]{1,0:T(8,128)(2,1)S(1)}, bf16[400,128]{1,0:T(8,128)(2,1)S(1)}, u32[]{:S(2)}, u32[]{:S(2)}) collective-permute-start(bf16[400,128]{1,0:T(8,128)(2,1)S(1)} %add_convert_fusion.2), channel_id=1, source_target_pairs={{0,4},{1,5},{2,6},{3,7},{4,0},{5,1},{6,2},{7,3},{8,12},{9,13},{10,... | collective-permute-start | bytes 307208 | tf_op jit(solution)/shard_map/ppermute | solution.py:499
  73.2 5.5 %collective-permute-start.10 = (bf16[400,128]{1,0:T(8,128)(2,1)S(1)}, bf16[400,128]{1,0:T(8,128)(2,1)S(1)}, u32[]{:S(2)}, u32[]{:S(2)}) collective-permute-start(bf16[400,128]{1,0:T(8,128)(2,1)S(1)} %add_convert_fusion.1), channel_id=1, source_target_pairs={{0,8},{1,9},{2,10},{3,11},{4,12},{5,13},{6,14},{7,15},{8,0},{9,1},... | collective-permute-start | bytes 307208 | tf_op jit(solution)/shard_map/ppermute | solution.py:499
  78.7 5.1 %collective-permute-start.11 = (bf16[400,128]{1,0:T(8,128)(2,1)S(1)}, bf16[400,128]{1,0:T(8,128)(2,1)S(1)}, u32[]{:S(2)}, u32[]{:S(2)}) collective-permute-start(bf16[400,128]{1,0:T(8,128)(2,1)S(1)} %add_convert_fusion), channel_id=1, source_target_pairs={{0,1},{1,0},{2,3},{3,2},{4,5},{5,4},{6,7},{7,6},{8,9},{9,8},{10,11... | collective-permute-start | bytes 307208 | tf_op jit(solution)/shard_map/ppermute | solution.py:499

commit v3 on v2

--- a/solution.py
+++ b/solution.py
@@ -15,8 +15,8 @@
 LANES = 128
 KEYS = 3 * LANES
 EDGE = HALO
-SUB = EDGE // 2
 FRAME = EDGE + 2 * WIN
+WIDE = -(-FRAME // LANES) * LANES
 SCORE_ROWS = 144
 CHUNK = 512
 SOFT = 0.1 * 0.1
@@ -53,9 +53,9 @@
         vz[:, :, h, :, LANES:] = jnp.broadcast_to(mask.reshape(1, 1, 1, LANES), shape)
 
 
-def distances(offset):
-    qpos = lax.broadcasted_iota(jnp.int32, (WIN, KEYS), 0) + offset
-    return jnp.abs(qpos - lax.broadcasted_iota(jnp.int32, (WIN, KEYS), 1))
+def distances(rows, keys, offset):
+    qpos = lax.broadcasted_iota(jnp.int32, (rows, keys), 0) + offset
+    return jnp.abs(qpos - lax.broadcasted_iota(jnp.int32, (rows, keys), 1))
 
 
 def take(ref, *at):
@@ -69,22 +69,22 @@
 def attend_all(blocks, kz, vz, beside=()):
     def score(block):
         q, m, p, start = block[:4]
-        window = pl.ds(start, KEYS)
+        window = pl.ds(start, block[7])
         keys = jnp.concatenate([kz[m, p, 0, window, :], kz[m, p, 1, window, :]], axis=0)
         return lax.dot_general(q(), keys, NT, preferred_element_type=F32)
 
     def soften(logits, block):
-        away, reach = block[4](), block[5]
+        away, reach, count = block[4](), block[5], block[7]
         parts = []
         for h in range(2):
-            one = jnp.where(away <= reach[h], logits[:, h * KEYS : (h + 1) * KEYS], NEG)
+            one = jnp.where(away <= reach[h], logits[:, h * count : (h + 1) * count], NEG)
             peak = jnp.max(one, axis=1, keepdims=True)
             parts.append(jnp.exp(one - peak).astype(BF16))
         return jnp.concatenate(parts, axis=1)
 
     def finish(probs, block):
         m, p, start = block[1:4]
-        window = pl.ds(start, KEYS)
+        window = pl.ds(start, block[7])
         values = jnp.concatenate([vz[m, p, 0, window, :], vz[m, p, 1, window, :]], axis=0)
         mixed = mm(probs, values)
         block[6]((mixed[:, :LANES] / mixed[:, LANES:]).astype(BF16))
@@ -105,8 +105,8 @@
 
 
 def main_kernel(
-    scale, info, x, xh, wq, wk, wv, wo_hbm, dec, q_out, k_out, v_out, hid, fc,
-    kz0, vz0, qs0, kz1, vz1, qs1, att, res, far, wo, sem,
+    scale, info, x, xh, wq, wk, wv, wo_hbm, dec, truth, q_out, k_out, v_out, hid, fc, truth_t, t_near, t_far,
+    kz0, vz0, qs0, kz1, vz1, qs1, att, res, far, far_edge, wo, sem, wide,
 ):
     step = pl.program_id(0)
     members, own, width = x.shape
@@ -118,6 +118,7 @@
     halo_at = jnp.where(lower, 0, HALO + own)
     near = jnp.where(lower, WIN, 0)
     edge = jnp.where(lower, 0, own - WIN + MARGIN)
+    window_at = jnp.minimum(edge, own + 2 * HALO - WIDE)
     halo_rows = pl.ds(pl.multiple_of(halo_at, 32), HALO)
     near_from = pl.ds(pl.multiple_of(near, 32), MARGIN)
     near_at = pl.ds(pl.multiple_of(halo_at + near, 32), MARGIN)
@@ -174,33 +175,41 @@
                             m,
                             p,
                             first - WIN,
-                            functools.partial(take, far, 0, slice(None), slice(None)),
+                            functools.partial(take, far, slice(None), slice(None)),
                             reach,
                             functools.partial(keep, att, m, pl.ds(b * WIN, WIN), out_lanes),
+                            KEYS,
                         )
                     )
-                for b in range(2):
-                    q_rows = pl.ds(pl.multiple_of(edge + WIN + b * SUB, 16), SUB)
-                    blocks.append(
-                        (
-                            functools.partial(take, qs, m, q_rows, lanes),
-                            m,
-                            p,
-                            pl.multiple_of(edge + b * (FRAME - KEYS), 32),
-                            functools.partial(take, far, b, slice(0, SUB), slice(None)),
-                            reach,
-                            functools.partial(keep, att, m, pl.ds(inner + b * SUB, SUB), out_lanes),
-                        )
+                blocks.append(
+                    (
+                        functools.partial(take, qs, m, pl.ds(pl.multiple_of(edge + WIN, 32), EDGE), lanes),
+                        m,
+                        p,
+                        pl.multiple_of(window_at, 32),
+                        functools.partial(take, far_edge, slice(None), slice(None)),
+                        reach,
+                        functools.partial(keep, att, m, pl.ds(inner, EDGE), out_lanes),
+                        WIDE,
                     )
+                )
         attend_all(blocks, kz, vz, beside)
 
     @pl.when(step == 0)
     def _():
         weight_copy.start()
+        channels = truth.shape[0]
+        wide[:channels, :] = truth[...]
+        wide[channels:, :] = jnp.zeros((LANES - channels, own), F32)
+        for tile in range(own // LANES):
+            tokens = slice(tile * LANES, (tile + 1) * LANES)
+            truth_t[tokens, :] = wide[:, tokens].T
+        t_near[...] = truth_t[pl.ds(pl.multiple_of(jnp.where(lower, 0, own - MARGIN), 32), MARGIN), :]
+        t_far[...] = truth_t[pl.ds(pl.multiple_of(jnp.where(lower, own - MARGIN, 0), 32), MARGIN), :]
         for _, vz, _ in sets:
             put_ones(vz, pairs)
-        for b in range(2):
-            far[b] = distances(WIN + b * (SUB + KEYS - FRAME))
+        far[...] = distances(WIN, KEYS, WIN)
+        far_edge[...] = distances(EDGE, WIDE, edge + WIN - window_at)
         for work in projections(*sets[0]):
             work()
 
@@ -277,18 +286,18 @@
             lanes = slice(p * LANES, (p + 1) * LANES)
             out_lanes = pl.ds(pl.multiple_of(group * cols + p * LANES, LANES), LANES)
             for m in range(members):
-                for b in range(2):
-                    blocks.append(
-                        (
-                            functools.partial(take, qs, m, pl.ds(b * SUB, SUB), lanes),
-                            m,
-                            p,
-                            b * (FRAME - KEYS),
-                            functools.partial(take, far, b, slice(0, SUB), slice(None)),
-                            reach,
-                            functools.partial(keep, att, m, pl.ds(b * SUB, SUB), out_lanes),
-                        )
+                blocks.append(
+                    (
+                        functools.partial(take, qs, m, slice(None), lanes),
+                        m,
+                        p,
+                        0,
+                        functools.partial(take, far, slice(None), slice(None)),
+                        reach,
+                        functools.partial(keep, att, m, slice(None), out_lanes),
+                        WIDE,
                     )
+                )
         attend_all(blocks, kz, vz, beside)
 
     @pl.when(step == 0)
@@ -296,11 +305,11 @@
         weight_copy.start()
         for _, vz, _ in sets:
             put_ones(vz, pairs)
-        for b in range(2):
-            start = b * (FRAME - KEYS)
-            kpos = lax.broadcasted_iota(jnp.int32, (WIN, KEYS), 1) + start
-            away = distances(WIN + b * SUB - start)
-            far[b] = jnp.where((kpos >= low) & (kpos < high), away, 1 << 20)
+        for kz, vz, _ in sets:
+            kz[:, :, :, FRAME:, :] = jnp.zeros((members, pairs, 2, WIDE - FRAME, LANES), BF16)
+            vz[:, :, :, FRAME:, :LANES] = jnp.zeros((members, pairs, 2, WIDE - FRAME, LANES), BF16)
+        kpos = lax.broadcasted_iota(jnp.int32, (EDGE, WIDE), 1)
+        far[...] = jnp.where((kpos >= low) & (kpos < high), distances(EDGE, WIDE, WIN), 1 << 20)
         for work in projections(*sets[0]):
             work()
 
@@ -347,7 +356,7 @@
 
 
 def score_kernel(
-    channels, members_total, info, radii, fa, fb, ga, gb, truth, t_near, t_far, hid_a, hid_b, cot, part, fh, fl, sh, sl
+    channels, members_total, info, radii, fa, fb, ga, gb, truth, t_near, t_far, hid_a, hid_b, cot, mine, theirs, fh, fl, sh, sl
 ):
     members, _, _ = fa.shape
     own = truth.shape[0]
@@ -441,8 +450,8 @@
                 slope = (slopes[m] * (1.0 / members_total) - pair_weight * cross[m]) * valid
                 keep, lanes = pl.ds(tile * rows, rows), slice(m * LANES, (m + 1) * LANES)
                 sh[s, keep, lanes], sl[s, keep, lanes] = split(slope)
-        mine = (line >= RMAX) & (line < RMAX + own)
-        total = total + jnp.where(mine, tile_score, 0.0)
+        scored = (line >= RMAX) & (line < RMAX + own)
+        total = total + jnp.where(scored, tile_score, 0.0)
     lane = lax.broadcasted_iota(jnp.int32, (rows, LANES), 1)
     total = jnp.where(lane < channels, total, 0.0)
     score = jnp.sum(jnp.sum(total, axis=0, keepdims=True), axis=1, keepdims=True)
@@ -468,16 +477,32 @@
             (far_own, hid_b, pl.ds(far_skip, WIN)),
         ):
             grad = grad + lax.dot_general(cot[c_rows, lanes], ref[m, h_rows, :], TN, preferred_element_type=F32)
-    chunks = width // LANES // part.shape[0]
-    extra = part.shape[1] - chunks * channels
+    chunks = width // LANES // 2
+    extra = mine.shape[0] - chunks * channels
     line = lax.broadcasted_iota(jnp.int32, (extra, LANES), 0)
     score_high = score.astype(BF16).astype(F32)
     tail = jnp.where(line == 0, score_high, jnp.where(line == 1, score - score_high, 0.0)).astype(BF16)
-    for h in range(part.shape[0]):
-        for c in range(chunks):
-            first = (h * chunks + c) * LANES
-            part[h, c * channels : (c + 1) * channels, :] = grad[:channels, first : first + LANES].astype(BF16)
-        part[h, chunks * channels :, :] = tail
+    for c in range(chunks):
+        low_part = grad[:channels, c * LANES : (c + 1) * LANES].astype(BF16)
+        high_part = grad[:channels, (chunks + c) * LANES : (chunks + c + 1) * LANES].astype(BF16)
+        rows_at = slice(c * channels, (c + 1) * channels)
+        mine[rows_at, :] = jnp.where(lower, low_part, high_part)
+        theirs[rows_at, :] = jnp.where(lower, high_part, low_part)
+    mine[chunks * channels :, :] = tail
+    theirs[chunks * channels :, :] = tail
+
+
+def assemble_kernel(scale_grad, scale_score, total, other, grad, score):
+    channels = grad.shape[0]
+    chunks = grad.shape[1] // LANES // 2
+    even = lax.axis_index("band") % 2 == 0
+    for c in range(chunks):
+        rows = slice(c * channels, (c + 1) * channels)
+        ours, others = total[rows, :].astype(F32) * scale_grad, other[rows, :].astype(F32) * scale_grad
+        grad[:, c * LANES : (c + 1) * LANES] = jnp.where(even, ours, others)
+        grad[:, (chunks + c) * LANES : (chunks + c + 1) * LANES] = jnp.where(even, others, ours)
+    terms = total[chunks * channels :, :].astype(F32)
+    score[0, 0] = (terms[0, 0] + terms[1, 0]) * scale_score
 
 
 def grad_kernel(cot, dec, out):
@@ -491,9 +516,8 @@
     return pairs
 
 
-def reduce_all(part, mesh_shape, beside):
+def reduce_all(mine, theirs, mesh_shape, beside):
     bands, count = mesh_shape["band"], mesh_shape["member"]
-    core = lax.axis_index("band") % 2
 
     def swap(values, axis, size, bit):
         return lax.ppermute(values, axis, [(i, i ^ bit) for i in range(size)])
@@ -501,22 +525,18 @@
     def add(mine, theirs):
         return (mine.astype(F32) + theirs.astype(F32)).astype(BF16)
 
-    theirs = lax.dynamic_index_in_dim(part, 1 - core, 0, keepdims=False)
-    mine = lax.dynamic_index_in_dim(part, core, 0, keepdims=False)
     total = add(mine, swap(theirs, "band", bands, 1))
     steps = [("member", count, 1 << i) for i in range(count.bit_length() - 1)]
     steps += [("band", bands, 1 << i) for i in range(1, bands.bit_length() - 1)]
     aside = None
     for i, (axis, size, bit) in enumerate(steps):
         got = swap(total, axis, size, bit)
-        if i == 0:
+        if i == len(steps) - 1:
             aside = beside(total)
             got, aside = lax.optimization_barrier((got, aside))
         total = add(total, got)
     other = swap(total, "band", bands, 1)
-    low = jnp.where(core == 0, total, other)
-    high = jnp.where(core == 0, other, total)
-    return jnp.stack([low, high]).astype(F32), aside
+    return total, other, aside
 
 
 def local(mesh_shape, fields, w_qkv, w_out, decoder_weight, window_reach, truth, radii):
@@ -539,15 +559,9 @@
     inside = swap_pairs(bands, 0)
     across = swap_pairs(bands, 1) + [(0, 0), (bands - 1, bands - 1)]
 
-    def exchange(block, dim, size):
-        last = block.shape[dim] - size
-        near = lax.dynamic_slice_in_dim(block, (1 - core) * last, size, dim)
-        far = lax.dynamic_slice_in_dim(block, core * last, size, dim)
-        return lax.ppermute(near, "band", inside), lax.ppermute(far, "band", across)
-
-    x_near, x_far = exchange(fields, 1, HALO)
-    truth_t = jnp.pad(truth.T, ((0, 0), (0, LANES - channels)))
-    t_near, t_far = exchange(truth_t, 0, MARGIN)
+    last = own - HALO
+    x_near = lax.ppermute(lax.dynamic_slice_in_dim(fields, (1 - core) * last, HALO, 1), "band", inside)
+    x_far = lax.ppermute(lax.dynamic_slice_in_dim(fields, core * last, HALO, 1), "band", across)
     dec = jnp.pad(decoder_weight, ((0, LANES - channels), (0, 0)))
 
     cols = 2 * LANES
@@ -569,7 +583,7 @@
         pltpu.VMEM((members, pairs, 2, own + 2 * HALO, 2 * LANES), BF16),
         pltpu.VMEM((members, own + 2 * HALO, cols), BF16),
     ]
-    q_own, k_own, v_own, hid_a, fc_a = pl.pallas_call(
+    q_own, k_own, v_own, hid_a, fc_a, truth_t, t_near, t_far = pl.pallas_call(
         functools.partial(main_kernel, scale),
         grid_spec=pltpu.PrefetchScalarGridSpec(
             num_scalar_prefetch=1,
@@ -582,6 +596,7 @@
                 group_weight(2),
                 pl.BlockSpec(memory_space=pl.ANY),
                 whole((LANES, width)),
+                whole((channels, own)),
             ],
             out_specs=[
                 group_block(own),
@@ -589,26 +604,34 @@
                 group_block(own),
                 whole((members, main_rows, width)),
                 whole((members, main_rows, LANES)),
+                whole((own, LANES)),
+                whole((MARGIN, LANES)),
+                whole((MARGIN, LANES)),
             ],
             scratch_shapes=work_set * 2
             + [
                 pltpu.VMEM((members, main_rows, width), BF16),
                 pltpu.VMEM((EDGE, width), BF16),
-                pltpu.VMEM((2, WIN, KEYS), jnp.int32),
+                pltpu.VMEM((WIN, KEYS), jnp.int32),
+                pltpu.VMEM((EDGE, WIDE), jnp.int32),
                 pltpu.VMEM((width, width), BF16),
                 pltpu.SemaphoreType.DMA,
+                pltpu.VMEM((LANES, own), F32),
             ],
         ),
         out_shape=[jax.ShapeDtypeStruct((members, own, width), BF16)] * 3
         + [
             jax.ShapeDtypeStruct((members, main_rows, width), BF16),
             jax.ShapeDtypeStruct((members, main_rows, LANES), F32),
+            jax.ShapeDtypeStruct((own, LANES), F32),
+            jax.ShapeDtypeStruct((MARGIN, LANES), F32),
+            jax.ShapeDtypeStruct((MARGIN, LANES), F32),
         ],
         compiler_params=params,
         cost_estimate=pl.CostEstimate(
             flops=2 * members * own * width * 5 * width, bytes_accessed=24 << 20, transcendentals=1 << 22
         ),
-    )(info, fields, x_near, w_qkv, w_qkv, w_qkv, w_out, dec)
+    )(info, fields, x_near, w_qkv, w_qkv, w_qkv, w_out, dec, truth)
 
     member_pairs = [(i, i ^ 1) for i in range(member_count)]
     other_a = lax.ppermute(fc_a, "member", member_pairs)
@@ -635,15 +658,15 @@
             ],
             out_specs=[whole((members, EDGE, width)), whole((members, EDGE, LANES))],
             scratch_shapes=[
-                pltpu.VMEM((members, pairs, 2, FRAME, LANES), BF16),
-                pltpu.VMEM((members, pairs, 2, FRAME, 2 * LANES), BF16),
+                pltpu.VMEM((members, pairs, 2, WIDE, LANES), BF16),
+                pltpu.VMEM((members, pairs, 2, WIDE, 2 * LANES), BF16),
                 pltpu.VMEM((members, EDGE, cols), BF16),
             ]
             * 2
             + [
                 pltpu.VMEM((members, EDGE, width), BF16),
                 pltpu.VMEM((members, EDGE, width), BF16),
-                pltpu.VMEM((2, WIN, KEYS), jnp.int32),
+                pltpu.VMEM((EDGE, WIDE), jnp.int32),
                 pltpu.VMEM((width, width), BF16),
                 pltpu.SemaphoreType.DMA,
             ],
@@ -658,6 +681,8 @@
         ),
     )(info, fields, x_far, w_qkv, w_qkv, w_qkv, q_own, k_own, v_own, w_out, dec)
     other_b = lax.ppermute(fc_b, "member", member_pairs)
+    t_near = lax.ppermute(t_near, "band", inside)
+    t_far = lax.ppermute(t_far, "band", across)
 
     chunks = width // LANES // 2
     keep_rows = chunks * channels + 16
@@ -666,13 +691,14 @@
     s_rows = own + LANES
     smem = pl.BlockSpec(memory_space=pltpu.SMEM)
     vmem = pl.BlockSpec(memory_space=pltpu.VMEM)
-    cot, part = pl.pallas_call(
+    cot, mine, theirs = pl.pallas_call(
         functools.partial(score_kernel, channels, members_total),
         in_specs=[smem, smem] + [vmem] * 9,
-        out_specs=[vmem, vmem],
+        out_specs=[vmem, vmem, vmem],
         out_shape=[
             jax.ShapeDtypeStruct((own, members * LANES), BF16),
-            jax.ShapeDtypeStruct((2, keep_rows, LANES), BF16),
+            jax.ShapeDtypeStruct((keep_rows, LANES), BF16),
+            jax.ShapeDtypeStruct((keep_rows, LANES), BF16),
         ],
         scratch_shapes=[
             pltpu.VMEM((f_rows, (2 * members + 1) * LANES), BF16),
@@ -688,6 +714,7 @@
         return pl.pallas_call(
             grad_kernel,
             grid=(members, 2),
+            compiler_params=pltpu.CompilerParams(vmem_limit_bytes=16 * 1024 * 1024),
             in_specs=[
                 pl.BlockSpec((own // 2, LANES), lambda m, h: (h, m)),
                 pl.BlockSpec((LANES, width), lambda m, h: (0, 0)),
@@ -699,12 +726,19 @@
             ),
         )(cot_now, dec)
 
-    summed, hidden_grad = reduce_all(part, mesh_shape, pull_back)
-    decoder_grad = summed[:, : chunks * channels].reshape(2 * chunks, channels, LANES)
-    decoder_grad = decoder_grad.transpose(1, 0, 2).reshape(channels, width)
-    decoder_grad = decoder_grad / math.sqrt(members_total * own * bands)
-    score = summed[0, chunks * channels, 0] + summed[0, chunks * channels + 1, 0]
-    mean_score = score / (scales * channels * own * bands)
+    total, other, hidden_grad = reduce_all(mine, theirs, mesh_shape, pull_back)
+    decoder_grad, mean_score = pl.pallas_call(
+        functools.partial(
+            assemble_kernel,
+            1.0 / math.sqrt(members_total * own * bands),
+            1.0 / (scales * channels * own * bands),
+        ),
+        in_specs=[vmem, vmem],
+        out_specs=[vmem, smem],
+        out_shape=[jax.ShapeDtypeStruct((channels, width), F32), jax.ShapeDtypeStruct((1, 1), F32)],
+        compiler_params=pltpu.CompilerParams(vmem_limit_bytes=16 * 1024 * 1024),
+    )(total, other)
+    mean_score = mean_score.reshape(())
     return (mean_score, decoder_grad, hidden_grad)
 
 

time: 88 us -> 81.6 us (0.927); the launches traced: 87.6 us -> 80.2 us
  local copies, waits for them, and re-layouts: 5.54 us -> 1.62 us
  between operations: 3.28 us -> 0.97 us
  Pallas kernels: 46.3 us -> 44.2 us
    unnamed x13 -> x10, local copies, waits for them, and re-layouts: 1.77 us -> 0.02 us
    dynamic_slice x2 -> x1, local copies, waits for them, and re-layouts: 2.33 us -> 1.49 us  [local(): lax.dynamic_slice_in_dim(fields, core * last, HALO, 1)]
    pallas_call x1 -> x2, Pallas kernels: 3.99 us -> 3.32 us  [the longest x1 2.5 us: pull_back(): pl.pallas_call(grad_kernel, grid=(members, 2), compiler_params=pltpu.Comp...]
  transfers between devices with their start and end apart: 12 -> 12, of which waited for: 6 -> 7; matrix products, arithmetic and copies ran while one was open for 1% -> 0% of each run, Pallas kernels for 46% -> 47%
where the time goes in v3:
time: 81.6 us; the launch traced here: 80.2 us
  Pallas kernels  44.2 us (54%)
  waiting for transfers between devices  17.6 us (22%)
  starting transfers between devices  15.7 us (19%)
  local copies, waits for them, and re-layouts  1.62 us (2%)
  between operations  0.97 us (1%)
    pallas_call x1, Pallas kernels, local(): pl.pallas_call(functools.partial(main_kernel, scale), grid_spec=pltpu.Pre...  24.4 us
    ppermute x6, waiting for transfers between devices, swap(): return lax.ppermute(values, axis, [(i, i ^ bit) for i in range(size)])  14.4 us
    pallas_call x1, Pallas kernels, local(): pl.pallas_call(functools.partial(edge_kernel, scale), grid_spec=pltpu.Pre...  10.7 us
    ppermute x6, starting transfers between devices, swap(): return lax.ppermute(values, axis, [(i, i ^ bit) for i in range(size)])  7.22 us
    pallas_call x1, Pallas kernels, local(): pl.pallas_call(functools.partial(score_kernel, channels, members_total),...  5.78 us
    ppermute x1, waiting for transfers between devices, local(): t_far = lax.ppermute(t_far, 'band', across)  3.17 us
    ppermute x1, starting transfers between devices, local(): lax.ppermute(lax.dynamic_slice_in_dim(fields, core * last, HALO, 1), 'ban...  3.02 us
    pallas_call x1, Pallas kernels, pull_back(): pl.pallas_call(grad_kernel, grid=(members, 2), compiler_params=pltpu.Comp...  2.5 us
  transfers between devices with their start and end apart: 12, of which 7 were waited for; matrix products, arithmetic and copies ran while one was open for 0% of the time, Pallas kernels for 47%

profile of v3, /device:TPU:25, one launch (start us, length us, event | category | flops | bytes accessed | tf_op | source)
XLA Modules:
  0.0 80.2 jit_solution(7290342984331155609)
XLA Ops:
  0.7 1.5 %constant_dynamic-slice_fusion = (bf16[2,160,1024]{2,1,0:T(8,128)(2,1)S(1)}, bf16[2,160,1024]{2,1,0:T(8,128)(2,1)S(1)}) fusion(bf16[2,512,1024]{2,1,0:T(8,128)(2,1)} %x.5, s32[]{:T(128)S(6)} %select_n.15, s32[]{:T(128)S(6)} %select_n.14), kind=kLoop, calls=%fused_computation.5 | loop fusion | bytes 2621448 | tf_op jit(solution)/shard_map/dynamic_slice | solution.py:564
  2.2 0.7 collective-permute-start
  2.9 3.0 %collective-permute-start.1 = (bf16[2,160,1024]{2,1,0:T(8,128)(2,1)S(1)}, bf16[2,160,1024]{2,1,0:T(8,128)(2,1)S(1)}, u32[]{:S(2)}, u32[]{:S(2)}) collective-permute-start(bf16[2,160,1024]{2,1,0:T(8,128)(2,1)S(1)} %get-tuple-element.39), channel_id=1, source_target_pairs={{1,2},{2,1},{3,4},{4,3},{5,6},{6,5},{7,8},{8,7},{9,10},{10,9},{11,... | collective-permute-start | bytes 1966088 | tf_op jit(solution)/shard_map/ppermute | solution.py:564
  6.0 0.0 copy-done.3
  6.0 0.1 concatenate.3.info
  6.1 0.0 collective-permute-done.xh
  6.1 24.4 %shard_map.94 = (bf16[2,512,1024]{2,1,0:T(8,128)(2,1)S(1)}, bf16[2,512,1024]{2,1,0:T(8,128)(2,1)}, bf16[2,512,1024]{2,1,0:T(8,128)(2,1)}, bf16[2,416,1024]{2,1,0...) custom-call(s32[20]{0:T(128)S(1)} %concatenate.3.info, ...), custom_call_target="tpu_custom_call" | custom-call | flops 10737418240 | bytes 25165824 | tf_op jit(solution)/shard_map/pallas_call | solution.py:586
  30.5 1.3 %collective-permute-start.2 = (f32[2,416,128]{2,1,0:T(8,128)S(1)}, f32[2,416,128]{2,1,0:T(8,128)S(1)}, u32[]{:S(2)}, u32[]{:S(2)}) collective-permute-start(f32[2,416,128]{2,1,0:T(8,128)S(1)} %get-tuple-element.21.fa), channel_id=1, source_target_pairs={{0,16},{16,0},{1,17},{17,1},{2,18},{18,2},{3,19},{19,3},{4,20},{20... | collective-permute-start | bytes 1277960 | tf_op jit(solution)/shard_map/ppermute | solution.py:637
  31.8 0.0 collective-permute-done.1.xh
  31.8 10.7 %shard_map.95 = (bf16[2,160,1024]{2,1,0:T(8,128)(2,1)S(1)}, f32[2,160,128]{2,1,0:T(8,128)S(1)}) custom-call(s32[20]{0:T(128)S(1)} %concatenate.3.info, bf16[2,512,1024]{2,1,0:T(8,128)(2,1)S(1)} %copy-done, bf16[2,160,1024]{2,1,0:T(8,128)(2,1)S(1)} %collective-permute-done.1.xh, bf16[1024,3072]{1,0:T(8,128)(2,1)} %wv.3, bf16[1024,3072]{1,0:T(8,128)(2,1)} %wv.3, ...), custom_call_target="tpu_custom_call" | custom-call | flops 4294967296 | bytes 14680064 | tf_op jit(solution)/shard_map/pallas_call | solution.py:642
  42.5 0.3 collective-permute-start.3
  42.8 0.9 %collective-permute-start.4 = (f32[32,128]{1,0:T(8,128)S(1)}, f32[32,128]{1,0:T(8,128)S(1)}, u32[]{:S(2)}, u32[]{:S(2)}) collective-permute-start(f32[32,128]{1,0:T(8,128)S(1)} %get-tuple-element.27), channel_id=1, source_target_pairs={{0,1},{1,0},{2,3},{3,2},{4,5},{5,4},{6,7},{7,6},{8,9},{9,8},{10,11... | collective-permute-start | bytes 49160 | tf_op jit(solution)/shard_map/ppermute | solution.py:684
  43.7 2.2 %collective-permute-start.5 = (f32[32,128]{1,0:T(8,128)S(1)}, f32[32,128]{1,0:T(8,128)S(1)}, u32[]{:S(2)}, u32[]{:S(2)}) collective-permute-start(f32[32,128]{1,0:T(8,128)S(1)} %get-tuple-element.28), channel_id=1, source_target_pairs={{1,2},{2,1},{3,4},{4,3},{5,6},{6,5},{7,8},{8,7},{9,10},{10,9},{11,... | collective-permute-start | bytes 49160 | tf_op jit(solution)/shard_map/ppermute | solution.py:685
  45.9 0.0 collective-permute-done.4.t_near
  45.9 3.2 %collective-permute-done.5.t_far = f32[32,128]{1,0:T(8,128)S(1)} collective-permute-done((f32[32,128]{1,0:T(8,128)S(1)}, f32[32,128]{1,0:T(8,128)S(1)}, u32[]{:S(2)}, u32[]{:S(2)}) %collective-permute-start.5) | collective-permute-done | bytes 16416 | tf_op jit(solution)/shard_map/ppermute | solution.py:685
  49.1 0.0 collective-permute-done.3.gb
  49.1 0.0 collective-permute-done.2.ga
  49.1 5.8 %shard_map.96 = (bf16[512,256]{1,0:T(8,128)(2,1)S(1)}, bf16[400,128]{1,0:T(8,128)(2,1)S(1)}, bf16[400,128]{1,0:T(8,128)(2,1)S(1)}) custom-call(s32[20]{0:T(128)S(1)} %concatenate.3.info, s32[3]{0:T(128)S(1)} %copy-done.1, f32[2,416,128]{2,1,0:T(8,128)S(1)} %get-tuple-element.21.fa, f32[2,160,128]{2,1,0:T(8,128)S(1)} %get-tuple-element.25.fb, ...), custom_call_target="tpu_custom_call" | custom-call | tf_op jit(solution)/shard_map/pallas_call | solution.py:694
  54.9 0.7 collective-permute-start.6
  55.5 0.9 %collective-permute-done.6 = bf16[400,128]{1,0:T(8,128)(2,1)S(1)} collective-permute-done((bf16[400,128]{1,0:T(8,128)(2,1)S(1)}, bf16[400,128]{1,0:T(8,128)(2,1)S(1)}, u32[]{:S(2)}, u32[]{:S(2)}) %collective-permute-start.6) | collective-permute-done | bytes 102432 | tf_op jit(solution)/shard_map/ppermute | solution.py:523
  56.5 1.3 %collective-permute-start.7 = (bf16[400,128]{1,0:T(8,128)(2,1)S(1)}, bf16[400,128]{1,0:T(8,128)(2,1)S(1)}, u32[]{:S(2)}, u32[]{:S(2)}) collective-permute-start(bf16[400,128]{1,0:T(8,128)(2,1)S(1)} %add_convert_fusion.4), channel_id=1, source_target_pairs={{0,16},{16,0},{1,17},{17,1},{2,18},{18,2},{3,19},{19,3},{4,20},{20... | collective-permute-start | bytes 307208 | tf_op jit(solution)/shard_map/ppermute | solution.py:523
  57.8 2.9 %collective-permute-done.7 = bf16[400,128]{1,0:T(8,128)(2,1)S(1)} collective-permute-done((bf16[400,128]{1,0:T(8,128)(2,1)S(1)}, bf16[400,128]{1,0:T(8,128)(2,1)S(1)}, u32[]{:S(2)}, u32[]{:S(2)}) %collective-permute-start.7) | collective-permute-done | bytes 102432 | tf_op jit(solution)/shard_map/ppermute | solution.py:523
  60.7 0.1 collective-permute-start.8
  60.8 3.5 %collective-permute-done.8 = bf16[400,128]{1,0:T(8,128)(2,1)S(1)} collective-permute-done((bf16[400,128]{1,0:T(8,128)(2,1)S(1)}, bf16[400,128]{1,0:T(8,128)(2,1)S(1)}, u32[]{:S(2)}, u32[]{:S(2)}) %collective-permute-start.8) | collective-permute-done | bytes 102432 | tf_op jit(solution)/shard_map/ppermute | solution.py:523
  64.3 0.2 collective-permute-start.9
  64.6 3.3 %collective-permute-done.9 = bf16[400,128]{1,0:T(8,128)(2,1)S(1)} collective-permute-done((bf16[400,128]{1,0:T(8,128)(2,1)S(1)}, bf16[400,128]{1,0:T(8,128)(2,1)S(1)}, u32[]{:S(2)}, u32[]{:S(2)}) %collective-permute-start.9) | collective-permute-done | bytes 102432 | tf_op jit(solution)/shard_map/ppermute | solution.py:523
  67.9 0.1 collective-permute-start.10
  68.1 2.5 %shard_map.97 = bf16[2,512,1024]{2,1,0:T(8,128)(2,1)} custom-call(bf16[512,256]{1,0:T(8,128)(2,1)S(1)} %get-tuple-element.34.cot, bf16[128,1024]{1,0:T(8,128)(2,1)S(1)} %pad.4.dec), custom_call_target="tpu_custom_call" | custom-call | flops 268435456 | bytes 8388608 | tf_op jit(solution)/shard_map/pallas_call | solution.py:714
  70.6 2.8 %collective-permute-done.10 = bf16[400,128]{1,0:T(8,128)(2,1)S(1)} collective-permute-done((bf16[400,128]{1,0:T(8,128)(2,1)S(1)}, bf16[400,128]{1,0:T(8,128)(2,1)S(1)}, u32[]{:S(2)}, u32[]{:S(2)}) %collective-permute-start.10) | collective-permute-done | bytes 102432 | tf_op jit(solution)/shard_map/ppermute | solution.py:523
  73.4 4.8 %collective-permute-start.11 = (bf16[400,128]{1,0:T(8,128)(2,1)S(1)}, bf16[400,128]{1,0:T(8,128)(2,1)S(1)}, u32[]{:S(2)}, u32[]{:S(2)}) collective-permute-start(bf16[400,128]{1,0:T(8,128)(2,1)S(1)} %add_convert_fusion.total), channel_id=1, source_target_pairs={{0,1},{1,0},{2,3},{3,2},{4,5},{5,4},{6,7},{7,6},{8,9},{9,8},{10,11... | collective-permute-start | bytes 307208 | tf_op jit(solution)/shard_map/ppermute | solution.py:523
  78.3 0.9 %collective-permute-done.11.other = bf16[400,128]{1,0:T(8,128)(2,1)S(1)} collective-permute-done((bf16[400,128]{1,0:T(8,128)(2,1)S(1)}, bf16[400,128]{1,0:T(8,128)(2,1)S(1)}, u32[]{:S(2)}, u32[]{:S(2)}) %collective-permute-start.11) | collective-permute-done | bytes 102432 | tf_op jit(solution)/shard_map/ppermute | solution.py:523
  79.2 0.8 %shard_map.98 = (f32[96,1024]{1,0:T(8,128)}, f32[1,1]{1,0:T(1,128)}) custom-call(bf16[400,128]{1,0:T(8,128)(2,1)S(1)} %add_convert_fusion.total, bf16[400,128]{1,0:T(8,128)(2,1)S(1)} %collective-permute-done.11.other), custom_call_target="tpu_custom_call" | custom-call | tf_op jit(solution)/shard_map/pallas_call | solution.py:730
  (15 shorter events, 0.2 us)
Async XLA Ops:
  0.6 5.3 %copy-start.3 = (bf16[96,1024]{1,0:T(8,128)(2,1)S(1)}, bf16[96,1024]{1,0:T(8,128)(2,1)}, u32[]{:S(2)}) copy-start(bf16[96,1024]{1,0:T(8,128)(2,1)} %param.10) | copy-start | bytes 589828
  0.6 5.4 %copy-start.4 = (s32[16]{0:T(128)S(1)}, s32[16]{0:T(128)}, u32[]{:S(2)}) copy-start(s32[16]{0:T(128)} %param.11) | copy-start | bytes 196
  0.7 5.5 %copy-start.2 = (f32[96,512]{1,0:T(8,128)S(1)}, f32[96,512]{1,0:T(8,128)}, u32[]{:S(2)}) copy-start(f32[96,512]{1,0:T(8,128)} %truth.1) | copy-start | bytes 589828
  2.2 3.9 %collective-permute-start = (bf16[2,160,1024]{2,1,0:T(8,128)(2,1)S(1)}, bf16[2,160,1024]{2,1,0:T(8,128)(2,1)S(1)}, u32[]{:S(2)}, u32[]{:S(2)}) collective-permute-start(bf16[2,160,1024]{2,1,0:T(8,128)(2,1)S(1)} %get-tuple-element.40), channel_id=1, source_target_pairs={{0,1},{1,0},{2,3},{3,2},{4,5},{5,4},{6,7},{7,6},{8,9},{9,8},{10,11... | collective-permute-start | bytes 1966088 | tf_op jit(solution)/shard_map/ppermute | solution.py:563
  2.9 28.9 %collective-permute-start.1 = (bf16[2,160,1024]{2,1,0:T(8,128)(2,1)S(1)}, bf16[2,160,1024]{2,1,0:T(8,128)(2,1)S(1)}, u32[]{:S(2)}, u32[]{:S(2)}) collective-permute-start(bf16[2,160,1024]{2,1,0:T(8,128)(2,1)S(1)} %get-tuple-element.39), channel_id=1, source_target_pairs={{1,2},{2,1},{3,4},{4,3},{5,6},{6,5},{7,8},{8,7},{9,10},{10,9},{11,... | collective-permute-start | bytes 1966088 | tf_op jit(solution)/shard_map/ppermute | solution.py:564
  6.1 25.7 %copy-start = (bf16[2,512,1024]{2,1,0:T(8,128)(2,1)S(1)}, bf16[2,512,1024]{2,1,0:T(8,128)(2,1)}, u32[]{:S(2)}) copy-start(bf16[2,512,1024]{2,1,0:T(8,128)(2,1)} %x.5) | copy-start | bytes 6291460
  30.5 18.6 %collective-permute-start.2 = (f32[2,416,128]{2,1,0:T(8,128)S(1)}, f32[2,416,128]{2,1,0:T(8,128)S(1)}, u32[]{:S(2)}, u32[]{:S(2)}) collective-permute-start(f32[2,416,128]{2,1,0:T(8,128)S(1)} %get-tuple-element.21.fa), channel_id=1, source_target_pairs={{0,16},{16,0},{1,17},{17,1},{2,18},{18,2},{3,19},{19,3},{4,20},{20... | collective-permute-start | bytes 1277960 | tf_op jit(solution)/shard_map/ppermute | solution.py:637
  31.8 17.3 %copy-start.1 = (s32[3]{0:T(128)S(1)}, s32[3]{0:T(128)}, u32[]{:S(2)}) copy-start(s32[3]{0:T(128)} %radii.1) | copy-start | bytes 40
  42.5 6.6 %collective-permute-start.3 = (f32[2,160,128]{2,1,0:T(8,128)S(1)}, f32[2,160,128]{2,1,0:T(8,128)S(1)}, u32[]{:S(2)}, u32[]{:S(2)}) collective-permute-start(f32[2,160,128]{2,1,0:T(8,128)S(1)} %get-tuple-element.25.fb), channel_id=1, source_target_pairs={{0,16},{16,0},{1,17},{17,1},{2,18},{18,2},{3,19},{19,3},{4,20},{20... | collective-permute-start | bytes 491528 | tf_op jit(solution)/shard_map/ppermute | solution.py:683
  42.8 3.1 %collective-permute-start.4 = (f32[32,128]{1,0:T(8,128)S(1)}, f32[32,128]{1,0:T(8,128)S(1)}, u32[]{:S(2)}, u32[]{:S(2)}) collective-permute-start(f32[32,128]{1,0:T(8,128)S(1)} %get-tuple-element.27), channel_id=1, source_target_pairs={{0,1},{1,0},{2,3},{3,2},{4,5},{5,4},{6,7},{7,6},{8,9},{9,8},{10,11... | collective-permute-start | bytes 49160 | tf_op jit(solution)/shard_map/ppermute | solution.py:684
  43.7 5.3 %collective-permute-start.5 = (f32[32,128]{1,0:T(8,128)S(1)}, f32[32,128]{1,0:T(8,128)S(1)}, u32[]{:S(2)}, u32[]{:S(2)}) collective-permute-start(f32[32,128]{1,0:T(8,128)S(1)} %get-tuple-element.28), channel_id=1, source_target_pairs={{1,2},{2,1},{3,4},{4,3},{5,6},{6,5},{7,8},{8,7},{9,10},{10,9},{11,... | collective-permute-start | bytes 49160 | tf_op jit(solution)/shard_map/ppermute | solution.py:685
  54.9 1.6 %collective-permute-start.6 = (bf16[400,128]{1,0:T(8,128)(2,1)S(1)}, bf16[400,128]{1,0:T(8,128)(2,1)S(1)}, u32[]{:S(2)}, u32[]{:S(2)}) collective-permute-start(bf16[400,128]{1,0:T(8,128)(2,1)S(1)} %get-tuple-element.32), channel_id=1, source_target_pairs={{0,1},{1,0},{2,3},{3,2},{4,5},{5,4},{6,7},{7,6},{8,9},{9,8},{10,11... | collective-permute-start | bytes 307208 | tf_op jit(solution)/shard_map/ppermute | solution.py:523
  56.5 4.2 %collective-permute-start.7 = (bf16[400,128]{1,0:T(8,128)(2,1)S(1)}, bf16[400,128]{1,0:T(8,128)(2,1)S(1)}, u32[]{:S(2)}, u32[]{:S(2)}) collective-permute-start(bf16[400,128]{1,0:T(8,128)(2,1)S(1)} %add_convert_fusion.4), channel_id=1, source_target_pairs={{0,16},{16,0},{1,17},{17,1},{2,18},{18,2},{3,19},{19,3},{4,20},{20... | collective-permute-start | bytes 307208 | tf_op jit(solution)/shard_map/ppermute | solution.py:523
  60.7 3.6 %collective-permute-start.8 = (bf16[400,128]{1,0:T(8,128)(2,1)S(1)}, bf16[400,128]{1,0:T(8,128)(2,1)S(1)}, u32[]{:S(2)}, u32[]{:S(2)}) collective-permute-start(bf16[400,128]{1,0:T(8,128)(2,1)S(1)} %add_convert_fusion.3), channel_id=1, source_target_pairs={{0,2},{1,3},{2,0},{3,1},{4,6},{5,7},{6,4},{7,5},{8,10},{9,11},{10,... | collective-permute-start | bytes 307208 | tf_op jit(solution)/shard_map/ppermute | solution.py:523
  64.3 3.6 %collective-permute-start.9 = (bf16[400,128]{1,0:T(8,128)(2,1)S(1)}, bf16[400,128]{1,0:T(8,128)(2,1)S(1)}, u32[]{:S(2)}, u32[]{:S(2)}) collective-permute-start(bf16[400,128]{1,0:T(8,128)(2,1)S(1)} %add_convert_fusion.2), channel_id=1, source_target_pairs={{0,4},{1,5},{2,6},{3,7},{4,0},{5,1},{6,2},{7,3},{8,12},{9,13},{10,... | collective-permute-start | bytes 307208 | tf_op jit(solution)/shard_map/ppermute | solution.py:523
  67.9 5.5 %collective-permute-start.10 = (bf16[400,128]{1,0:T(8,128)(2,1)S(1)}, bf16[400,128]{1,0:T(8,128)(2,1)S(1)}, u32[]{:S(2)}, u32[]{:S(2)}) collective-permute-start(bf16[400,128]{1,0:T(8,128)(2,1)S(1)} %add_convert_fusion.1), channel_id=1, source_target_pairs={{0,8},{1,9},{2,10},{3,11},{4,12},{5,13},{6,14},{7,15},{8,0},{9,1},... | collective-permute-start | bytes 307208 | tf_op jit(solution)/shard_map/ppermute | solution.py:523
  73.4 5.8 %collective-permute-start.11 = (bf16[400,128]{1,0:T(8,128)(2,1)S(1)}, bf16[400,128]{1,0:T(8,128)(2,1)S(1)}, u32[]{:S(2)}, u32[]{:S(2)}) collective-permute-start(bf16[400,128]{1,0:T(8,128)(2,1)S(1)} %add_convert_fusion.total), channel_id=1, source_target_pairs={{0,1},{1,0},{2,3},{3,2},{4,5},{5,4},{6,7},{7,6},{8,9},{9,8},{10,11... | collective-permute-start | bytes 307208 | tf_op jit(solution)/shard_map/ppermute | solution.py:523
